TPU v7x, 32 devices: a whole 2x2x4 slice. The times are simulated.
32 devices in a mesh: term: 16 (over z, y, x), sector: 2 (over core).
Axes of the slice: x: 2, y: 2, z: 4, core: 2. Of those that a mesh axis runs over, the one named last changes fastest.
Arguments:
- wave_blocks: bfloat16 [4, 512, 512], P(None, 'term'), may hold values from -0.59765625 to 0.59765625
- left_ops: bfloat16 [2, 32, 512, 512], P('sector', 'term'), may hold values from -0.25 to 0.25
- right_ops: bfloat16 [2, 64, 512, 512], P('sector', 'term'), may hold values from -0.25 to 0.25
- wanted: int32 [2, 16, 2], P('sector'), may hold values from 0 to 3, as said below
- pairs: int32 [2, 16, 12], P('sector', 'term'), may hold values from 0 to 15, as said below
- targets: int32 [2, 16, 12], P('sector', 'term'), may hold values from 0 to 1
- live: int32 [2, 16], P('sector', 'term'), may hold values from 1 to 12, as said below
Outputs:
- sigma: float32 [4, 512, 512], P('sector', 'term')
Inputs may be any that keep to these rules, and one draw needn't show every extreme that they name: `wanted`: the sectors listed for one section are distinct. `pairs`: codes are distinct within a section; a code c names half product c // 4 and right operator c % 4 of the section. Only the first live slots of a section are used; in every draw some section has 12 live slots.
All inputs are finite; a program needn't handle non-finite values.
Results may differ from a plain program's by a relative error of at most 0.0029.
Values may be sent and summed in bfloat16 or wider, within the bound.
No kernel may reach another device: no remote copies, remote signals or barrier semaphores. Data moves between devices by JAX's collectives and lax.ppermute only.
A program may use at most 64 MiB of HBM per device.

v0:
```python
import jax
import jax.numpy as jnp
from jax import lax
from jax.sharding import PartitionSpec as P

SEC_DEV = 2
OPS_R = 4


def on_device(wave_blocks, left_ops, right_ops, wanted, pairs, targets, live):
    section = lax.axis_index("term")
    block_size = left_ops.shape[2]
    gathered = lax.all_gather(wave_blocks, "term", axis=1, tiled=True)
    sources = lax.dynamic_index_in_dim(wanted[0], section, 0, keepdims=False)
    blocks = jnp.take(gathered, sources, axis=0)
    halves = jnp.einsum("aij,njk->anik", left_ops[0], blocks, preferred_element_type=jnp.float32)
    halves = halves.astype(jnp.bfloat16).reshape(-1, block_size, block_size)
    rights = right_ops[0]
    pair_codes = pairs[0, 0]
    slot_targets = targets[0, 0]

    def slot_step(slot, partial_value):
        pair_code = pair_codes[slot]
        half_pick = lax.dynamic_index_in_dim(halves, pair_code // OPS_R, 0, keepdims=False)
        right_pick = lax.dynamic_index_in_dim(rights, pair_code % OPS_R, 0, keepdims=False)
        product = lax.dot_general(
            half_pick, right_pick, (((1,), (1,)), ((), ())), preferred_element_type=jnp.float32
        )
        owner = slot_targets[slot]
        current = lax.dynamic_index_in_dim(partial_value, owner, 0, keepdims=False)
        return lax.dynamic_update_index_in_dim(partial_value, current + product, owner, 0)

    partial_value = jnp.zeros((SEC_DEV, block_size, block_size), jnp.float32)
    partial_value = lax.fori_loop(0, live[0, 0], slot_step, partial_value)
    sigma = lax.psum_scatter(partial_value, "term", scatter_dimension=1, tiled=True)
    return sigma


def solution(mesh):
    return jax.shard_map(
        on_device,
        mesh=mesh,
        in_specs=(
            P(None, "term", None),
            P("sector", "term", None, None),
            P("sector", "term", None, None),
            P("sector", None, None),
            P("sector", "term", None),
            P("sector", "term", None),
            P("sector", "term"),
        ),
        out_specs=P("sector", "term", None),
        check_vma=False,
    )
```

profile of v0, /device:TPU:0, one launch (start us, length us, event | category | flops | bytes accessed | tf_op | source)
XLA Modules:
  0.0 260.9 jit_solution(16879867020439015347)
XLA Ops:
  6.5 0.7 all-gather.2.cloned.1.call-update
  7.3 0.9 dynamic-slice_reduce_fusion
  8.2 65.5 %all-gather.2.cloned.1.call-done = bf16[4,512,512]{2,1,0:T(8,128)(2,1)} async-done(((bf16[4,32,512]{2,1,0:T(8,128)(2,1)}), bf16[4,512,512]{2,1,0:T(8,128)(2,1)}) %all-gather.2.cloned.1.call-update) | async-done | bytes 2097168 | tf_op jit(solution)/shard_map/all_gather | solution.py:13
  73.7 3.2 %gather_fusion = bf16[2,512,512]{2,1,0:T(8,128)(2,1)} fusion(bf16[4,512,512]{2,1,0:T(8,128)(2,1)} %all-gather.2.cloned.1.call-done, s32[1024]{0:T(1024)S(1)} %pad_clamp_fusion), kind=kCustom, calls=%fused_computation | custom fusion | bytes 2097160 | tf_op jit(solution)/shard_map/jit(_take)/gather | solution.py:15
  76.9 2.7 %convert_bitcast_fusion = bf16[2,2,512,512]{2,3,0,1:T(8,128)(2,1)S(1)} fusion(bf16[1,2,512,512]{3,2,1,0:T(8,128)(2,1)S(1)} %copy-done, bf16[2,512,512]{2,1,0:T(8,128)(2,1)} %gather_fusion, pred[2]{0:T(512)(128)(4,1)S(1)} %compare_and_fusion), kind=kOutput, calls=%fused_computation.10 | convolution fusion | flops 1075314688 | bytes 4194306 | tf_op jit(solution)/shard_map/aij,njk->anik/dot_general | solution.py:16
  79.6 2.4 copy.10
  82.6 76.4 %while.12 = (s32[]{:T(128)}, f32[2,512,512]{2,1,0:T(8,128)S(1)}, s32[]{:T(128)}, s32[12]{0:T(128)S(1)}, s32[12]{0:T(128)S(1)}, /*index=5*/bf16[4,512,512]{2,1,0:...) while((s32[]{:T(128)}, f32[2,512,512]{2,1,0:T(8,128)S(1)}, ...), condition=%wide.region_1.2_spmd, body=%wide.region_0.1_spmd.sunk | while | flops 268697632 | bytes 5243384 | solution.py:34
  85.6 0.6 dynamic_slice.56
  88.5 1.7 fusion.19
  93.1 0.6 dynamic_slice.56
  96.1 1.7 fusion.19
  100.7 0.6 dynamic_slice.56
  103.6 1.7 fusion.19
  111.2 1.7 fusion.19
  115.8 0.6 dynamic_slice.56
  118.8 1.7 fusion.19
  126.4 1.7 fusion.19
  133.9 1.7 fusion.19
  138.6 0.6 dynamic_slice.56
  141.5 1.7 fusion.19
  149.1 1.7 fusion.19
  156.6 1.7 fusion.19
  159.0 1.3 copy-done.1
  160.3 93.7 %reduce-scatter.2.cloned.1.call-done = f32[2,32,512]{2,1,0:T(8,128)} async-done(((f32[2,512,512]{2,1,0:T(8,128)}), f32[2,32,512]{2,1,0:T(8,128)}) %reduce-scatter.2.cloned.1.call-update) | async-done | bytes 131088 | tf_op jit(solution)/shard_map/reduce_scatter | solution.py:35
  (39 shorter events, 10.3 us)
Async XLA Ops:
  6.5 70.4 %copy-start = (bf16[1,2,512,512]{3,2,1,0:T(8,128)(2,1)S(1)}, bf16[1,2,512,512]{3,2,1,0:T(8,128)(2,1)}, u32[]{:S(2)}) copy-start(bf16[1,2,512,512]{3,2,1,0:T(8,128)(2,1)} %param.10) | copy-start | bytes 3145732
  6.5 67.2 %all-gather.2.cloned.1.call-start = ((), (), s32[]{:S(2)}) async-start(), calls=%async_computation.1 | async-start | bytes 2228224 | tf_op jit(solution)/shard_map/all_gather | solution.py:13
  7.3 246.8 %reduce-scatter.2.cloned.1.call-start = ((), (), s32[]{:S(2)}) async-start(), calls=%async_computation.2 | async-start | bytes 2228224 | tf_op jit(solution)/shard_map/reduce_scatter | solution.py:35
  81.9 0.7 copy-start.2
  82.0 0.7 copy-start.3
  159.0 1.3 copy-start.1
Sparse Core Ops, SparseCore 0:
  10.1 63.5 all-gather.1
  160.5 93.5 reduce-scatter.1
where the time goes:
time: 262 us; the launch traced here: 261 us
  waiting for transfers between devices  160 us (61%)
  loops' own time  47.2 us (18%)
  local copies, waits for them, and re-layouts  20.9 us (8%)
  matrix products  19.4 us (7%)
  between operations  13.4 us (5%)
    reduce_scatter x1, waiting for transfers between devices, on_device(): lax.psum_scatter(partial_value, 'term', scatter_dimension=1, tiled=True)  93.7 us
    all_gather x1, waiting for transfers between devices, on_device(): gathered = lax.all_gather(wave_blocks, 'term', axis=1, tiled=True)  65.5 us
    another operation x1, loops' own time, on_device(): partial_value = lax.fori_loop(0, live[0, 0], slot_step, partial_value)  47.2 us
    dot_general x10, matrix products, slot_step(): lax.dot_general(half_pick, right_pick, (((1,), (1,)), ((), ())), preferre...  16.8 us
    dynamic_slice x10, local copies, waits for them, and re-layouts, slot_step(): pair_code = pair_codes[slot]  5.84 us
    dynamic_slice x10, local copies, waits for them, and re-layouts, slot_step(): owner = slot_targets[slot]  5.82 us
  transfers between devices with their start and end apart: 2, of which 2 were waited for; matrix products, arithmetic and copies ran while one was open for 0% of the time, Pallas kernels for 0%

commit v1 on v0

v1 whole, which is shorter than its diff:
```python
import functools

import jax
import jax.numpy as jnp
from jax import lax
from jax.experimental import pallas as pl
from jax.experimental.pallas import tpu as pltpu
from jax.sharding import PartitionSpec as P

AXES = ("term", "sector")
BF16 = jnp.bfloat16
F32 = jnp.float32
VMEM = pl.BlockSpec(memory_space=pltpu.VMEM)
SMEM = pl.BlockSpec(memory_space=pltpu.SMEM)
VMEM_BYTES = 24 * 2**20


def block_owner(position, me, core, depth):
    quarter, level = position // depth, position % depth
    swapped = (0, 2, 1, 3)[quarter]
    near = jnp.where(core == 0, quarter, swapped)
    return lax.bitwise_xor(me, near + 4 * level)


def sigma_kernel(place, wanted, pairs, targets, live, mine, other, left, right,
                 keep0, send1, keep2, send3, wave, halves, total):
    devices, half_sectors, rows, size = mine.shape
    depth = devices // 4
    ops_l, ops_r, need = left.shape[1], right.shape[1], wave.shape[0]
    me, core = place[0], place[1]

    for j in range(need):
        source = wanted[0, me, j]
        owner_core = source // half_sectors
        local = source % half_sectors

        def unpack(blocks, from_core):
            for position in range(devices):
                start = block_owner(position, me, from_core, depth) * rows
                wave[j, pl.ds(pl.multiple_of(start, rows), rows), :] = blocks[position, local].astype(wave.dtype)

        @pl.when(owner_core == core)
        def _():
            unpack(mine, core)

        @pl.when(owner_core != core)
        def _():
            unpack(other, 1 - core)

    for a in range(ops_l):
        for j in range(need):
            product = jnp.dot(left[0, a], wave[j].astype(BF16), preferred_element_type=F32)
            halves[a * need + j] = product.astype(BF16)

    total[...] = jnp.zeros_like(total)

    def slot_step(slot, carry):
        code = pairs[0, 0, slot]
        target = targets[0, 0, slot]
        total[target] += lax.dot_general(
            halves[code // ops_r], right[0, code % ops_r], (((1,), (1,)), ((), ())), preferred_element_type=F32
        )
        return carry

    lax.fori_loop(0, live[0, 0], slot_step, 0)

    for quarter, out in enumerate((keep0, send1, keep2, send3)):
        for level in range(depth):
            start = block_owner(quarter * depth + level, me, core, depth) * rows
            for t in range(total.shape[0]):
                out[level, t] = total[t, pl.ds(pl.multiple_of(start, rows), rows), :].astype(out.dtype)


def on_device(terms, cores, wave_blocks, left_ops, right_ops, wanted, pairs, targets, live):
    sectors, rows, size = wave_blocks.shape
    me = lax.axis_index("term")
    core = lax.axis_index("sector") % 2
    depth = terms // 4
    sec_dev = sectors // cores
    need = wanted.shape[2]

    def swap(array, near, level=0):
        def partner(t, c):
            return t ^ (near[c % 2] + 4 * level)
        pairs_of = [(t * cores + c, partner(t, c) * cores + c) for t in range(terms) for c in range(cores)]
        return lax.ppermute(array, AXES, pairs_of)

    none, first, second = (0, 0), (1, 2), (2, 1)
    across = [(t * cores + c, t * cores + (c ^ 1)) for t in range(terms) for c in range(cores)]

    half = sectors // 2
    own = lax.dynamic_slice_in_dim(wave_blocks, core * half, half, 0)[None]
    line = jnp.concatenate([own] + [swap(own, none, k) for k in range(1, depth)], 0)
    from_first = swap(line, first)
    from_second = swap(line, second)
    from_both = swap(from_first, second)
    mine = jnp.concatenate([line, from_first, from_second, from_both], 0)
    other = lax.ppermute(mine, AXES, across)

    place = jnp.stack([me, core]).astype(jnp.int32)
    blocks = (depth, sec_dev, rows, size)
    wave_type = BF16 if rows % 16 == 0 else F32
    keep0, send1, keep2, send3 = pl.pallas_call(
        sigma_kernel,
        out_shape=[jax.ShapeDtypeStruct(blocks, t) for t in (F32, BF16, F32, BF16)],
        in_specs=[SMEM] * 5 + [VMEM] * 4,
        out_specs=[VMEM] * 4,
        scratch_shapes=[
            pltpu.VMEM((need, size, size), wave_type),
            pltpu.VMEM((left_ops.shape[1] * need, size, size), BF16),
            pltpu.VMEM((sec_dev, size, size), F32),
        ],
        compiler_params=pltpu.CompilerParams(vmem_limit_bytes=VMEM_BYTES),
        cost_estimate=pl.CostEstimate(flops=32 * size**3, bytes_accessed=12 * size * size * 2, transcendentals=0),
    )(place, wanted, pairs, targets, live, mine, other, left_ops, right_ops)

    far = swap(send3, first)
    near = swap(send1, first)
    passed = swap((keep2 + far.astype(F32)).astype(BF16), second)
    line_sum = keep0 + near.astype(F32) + passed.astype(F32)
    arrived = [swap(line_sum[k].astype(BF16), none, k) for k in range(1, depth)]
    sigma = line_sum[0]
    for part in arrived:
        sigma = sigma + part.astype(F32)
    return sigma


def solution(mesh):
    return jax.shard_map(
        functools.partial(on_device, mesh.shape["term"], mesh.shape["sector"]),
        mesh=mesh,
        in_specs=(
            P(None, "term", None),
            P("sector", "term", None, None),
            P("sector", "term", None, None),
            P("sector", None, None),
            P("sector", "term", None),
            P("sector", "term", None),
            P("sector", "term"),
        ),
        out_specs=P("sector", "term", None),
        check_vma=False,
    )
```

time: 262 us -> 63 us (0.24)
  waiting for transfers between devices: 160 us -> 34.5 us
  loops' own time: 47.2 us -> 0 us
  matrix products: 19.4 us -> 0 us
  local copies, waits for them, and re-layouts: 20.9 us -> 2.4 us
  starting transfers between devices: 0.04 us -> 15.2 us
  between operations: 13.4 us -> 0.77 us
  Pallas kernels: 0 us -> 8.46 us
    reduce_scatter x1 -> x0, waiting for transfers between devices: 93.7 us -> none  [on_device(): lax.psum_scatter(partial_value, 'term', scatter_dimension=1, tiled=True)]
    all_gather x1 -> x0, waiting for transfers between devices: 65.5 us -> none  [on_device(): gathered = lax.all_gather(wave_blocks, 'term', axis=1, tiled=True)]
    another operation x1 -> x0, loops' own time: 47.2 us -> none  [on_device(): partial_value = lax.fori_loop(0, live[0, 0], slot_step, partial_value)]
    ppermute x0 -> x13, waiting for transfers between devices: none -> 34.5 us  [the longest x12 32.6 us: swap(): return lax.ppermute(array, AXES, pairs_of)]
    dot_general x11 -> x0, matrix products: 19.4 us -> none  [the longest x10 16.8 us: slot_step(): lax.dot_general(half_pick, right_pick, (((1,), (1,)), ((), ())), preferre...]
    ppermute x0 -> x13, starting transfers between devices: none -> 15.2 us  [the longest x12 15.2 us: swap(): return lax.ppermute(array, AXES, pairs_of)]
    dynamic_slice x31 -> x0, local copies, waits for them, and re-layouts: 13.3 us -> none  [the longest x10 5.84 us: slot_step(): pair_code = pair_codes[slot]]
    pallas_call x0 -> x1, Pallas kernels: none -> 8.46 us  [on_device(): pl.pallas_call(sigma_kernel, out_shape=[jax.ShapeDtypeStruct(blocks, t) f...]
  transfers between devices with their start and end apart: 2 -> 13, of which waited for: 2 -> 11; matrix products, arithmetic and copies ran while one was open for 0% -> 0% of each run, Pallas kernels for 0% -> 0%
where the time goes in v1:
time: 63 us; the launch traced here: 62.4 us
  waiting for transfers between devices  34.5 us (55%)
  starting transfers between devices  15.2 us (24%)
  Pallas kernels  8.46 us (13%)
  local copies, waits for them, and re-layouts  2.4 us (4%)
  other arithmetic  0.99 us (2%)
  between operations  0.77 us (1%)
    ppermute x12, waiting for transfers between devices, swap(): return lax.ppermute(array, AXES, pairs_of)  32.6 us
    ppermute x12, starting transfers between devices, swap(): return lax.ppermute(array, AXES, pairs_of)  15.2 us
    pallas_call x1, Pallas kernels, on_device(): pl.pallas_call(sigma_kernel, out_shape=[jax.ShapeDtypeStruct(blocks, t) f...  8.46 us
    unnamed x17, local copies, waits for them, and re-layouts  2.37 us
    ppermute x1, waiting for transfers between devices, on_device(): other = lax.ppermute(mine, AXES, across)  1.96 us
  transfers between devices with their start and end apart: 13, of which 11 were waited for; matrix products, arithmetic and copies ran while one was open for 0% of the time, Pallas kernels for 0%

profile of v1, /device:TPU:0, one launch (start us, length us, event | category | flops | bytes accessed | tf_op | source)
XLA Modules:
  0.0 62.4 jit_solution(14273938401515056265)
XLA Ops:
  0.0 1.0 %constant_dynamic-update-slice_fusion.6 = (bf16[16,2,32,512]{3,2,1,0:T(8,128)(2,1)S(1)}, bf16[1,2,32,512]{3,2,1,0:T(8,128)(2,1)S(1)}) fusion(bf16[4,32,512]{2,1,0:T(8,128)(2,1)} %param.7, s32[]{:T(128)S(6)} %select_n.11), kind=kLoop, calls=%fused_computation.17 | loop fusion | bytes 196612
  1.0 5.1 %collective-permute-start.2 = (bf16[1,2,32,512]{3,2,1,0:T(8,128)(2,1)S(1)}, bf16[1,2,32,512]{3,2,1,0:T(8,128)(2,1)S(1)}, u32[]{:S(2)}, u32[]{:S(2)}) collective-permute-start(bf16[1,2,32,512]{3,2,1,0:T(8,128)(2,1)S(1)} %get-tuple-element.16), channel_id=1, source_target_pairs={{0,24},{1,25},{2,26},{3,27},{4,28},{5,29},{6,30},{7,31},{8,16},{9,... | collective-permute-start | bytes 196616 | tf_op jit(solution)/shard_map/ppermute | solution.py:86
  6.2 0.6 %collective-permute-start = (bf16[1,2,32,512]{3,2,1,0:T(8,128)(2,1)S(1)}, bf16[1,2,32,512]{3,2,1,0:T(8,128)(2,1)S(1)}, u32[]{:S(2)}, u32[]{:S(2)}) collective-permute-start(bf16[1,2,32,512]{3,2,1,0:T(8,128)(2,1)S(1)} %get-tuple-element.16), channel_id=1, source_target_pairs={{0,8},{1,9},{2,10},{3,11},{4,12},{5,13},{6,14},{7,15},{8,0},{9,1},... | collective-permute-start | bytes 196616 | tf_op jit(solution)/shard_map/ppermute | solution.py:86
  6.8 1.9 %collective-permute-done.2 = bf16[1,2,32,512]{3,2,1,0:T(8,128)(2,1)S(1)} collective-permute-done((bf16[1,2,32,512]{3,2,1,0:T(8,128)(2,1)S(1)}, bf16[1,2,32,512]{3,2,1,0:T(8,128)(2,1)S(1)}, u32[]{:S(2)}, u32[]{:S(2)}) %collective-permute-start.2) | collective-permute-done | bytes 65568 | tf_op jit(solution)/shard_map/ppermute | solution.py:86
  8.7 3.0 %collective-permute-done.1 = bf16[1,2,32,512]{3,2,1,0:T(8,128)(2,1)S(1)} collective-permute-done((bf16[1,2,32,512]{3,2,1,0:T(8,128)(2,1)S(1)}, bf16[1,2,32,512]{3,2,1,0:T(8,128)(2,1)S(1)}, u32[]{:S(2)}, u32[]{:S(2)}) %collective-permute-start.1) | collective-permute-done | bytes 65568 | tf_op jit(solution)/shard_map/ppermute | solution.py:86
  11.8 1.6 %collective-permute-start.3 = (bf16[4,2,32,512]{3,2,1,0:T(8,128)(2,1)S(1)}, bf16[4,2,32,512]{3,2,1,0:T(8,128)(2,1)S(1)}, u32[]{:S(2)}, u32[]{:S(2)}) collective-permute-start(bf16[4,2,32,512]{3,2,1,0:T(8,128)(2,1)S(1)} %pad_maximum_fusion), channel_id=1, source_target_pairs={{0,2},{1,5},{2,0},{3,7},{4,6},{5,1},{6,4},{7,3},{8,10},{9,13},{10,... | collective-permute-start | bytes 786440 | tf_op jit(solution)/shard_map/ppermute | solution.py:86
  13.4 1.5 %collective-permute-start.4 = (bf16[4,2,32,512]{3,2,1,0:T(8,128)(2,1)S(1)}, bf16[4,2,32,512]{3,2,1,0:T(8,128)(2,1)S(1)}, u32[]{:S(2)}, u32[]{:S(2)}) collective-permute-start(bf16[4,2,32,512]{3,2,1,0:T(8,128)(2,1)S(1)} %pad_maximum_fusion), channel_id=1, source_target_pairs={{0,4},{1,3},{2,6},{3,1},{4,0},{5,7},{6,2},{7,5},{8,12},{9,11},{10,... | collective-permute-start | bytes 786440 | tf_op jit(solution)/shard_map/ppermute | solution.py:86
  14.9 6.0 %collective-permute-done.3 = bf16[4,2,32,512]{3,2,1,0:T(8,128)(2,1)S(1)} collective-permute-done((bf16[4,2,32,512]{3,2,1,0:T(8,128)(2,1)S(1)}, bf16[4,2,32,512]{3,2,1,0:T(8,128)(2,1)S(1)}, u32[]{:S(2)}, u32[]{:S(2)}) %collective-permute-start.3) | collective-permute-done | bytes 262176 | tf_op jit(solution)/shard_map/ppermute | solution.py:86
  20.9 0.6 collective-permute-start.5
  21.6 5.7 %collective-permute-done.5 = bf16[4,2,32,512]{3,2,1,0:T(8,128)(2,1)S(1)} collective-permute-done((bf16[4,2,32,512]{3,2,1,0:T(8,128)(2,1)S(1)}, bf16[4,2,32,512]{3,2,1,0:T(8,128)(2,1)S(1)}, u32[]{:S(2)}, u32[]{:S(2)}) %collective-permute-start.5) | collective-permute-done | bytes 262176 | tf_op jit(solution)/shard_map/ppermute | solution.py:86
  28.2 2.0 %collective-permute-done.6.other = bf16[16,2,32,512]{3,2,1,0:T(8,128)(2,1)} collective-permute-done((bf16[16,2,32,512]{3,2,1,0:T(8,128)(2,1)S(1)}, bf16[16,2,32,512]{3,2,1,0:T(8,128)(2,1)}, u32[]{:S(2)}, u32[]{:S(2)}) %collective-permute-start.6) | collective-permute-done | bytes 1048608 | tf_op jit(solution)/shard_map/ppermute | solution.py:98
  30.2 1.2 %copy-done.1 = bf16[1,2,512,512]{3,2,1,0:T(8,128)(2,1)S(1)} copy-done((bf16[1,2,512,512]{3,2,1,0:T(8,128)(2,1)S(1)}, bf16[1,2,512,512]{3,2,1,0:T(8,128)(2,1)}, u32[]{:S(2)}) %copy-start.1) | copy-done | bytes 1048600
  31.4 8.5 %shard_map.73 = (f32[4,2,32,512]{3,2,1,0:T(8,128)S(1)}, bf16[4,2,32,512]{3,2,1,0:T(8,128)(2,1)S(1)}, f32[4,2,32,512]{3,2,1,0:T(8,128)S(1)}, bf16[4,2,32,512]{3,2,1,0:T(8,128)(2,1)S(1)}) custom-call(s32[2]{0:T(128)S(1)} %pad_add_fusion.place, s32[1,16,2]{2,1,0:T(8,128)S(1)} %copy.8.wanted, s32[1,1,12]{2,1,0:T(1,128)S(1)} %copy-done.2, ...), custom_call_target="tpu_custom_call" | custom-call | flops 4294967296 | bytes 6291456 | tf_op jit(solution)/shard_map/pallas_call | solution.py:103
  40.0 2.0 %collective-permute-start.7 = (bf16[4,2,32,512]{3,2,1,0:T(8,128)(2,1)S(1)}, bf16[4,2,32,512]{3,2,1,0:T(8,128)(2,1)S(1)}, u32[]{:S(2)}, u32[]{:S(2)}) collective-permute-start(bf16[4,2,32,512]{3,2,1,0:T(8,128)(2,1)S(1)} %get-tuple-element.10), channel_id=1, source_target_pairs={{0,2},{1,5},{2,0},{3,7},{4,6},{5,1},{6,4},{7,3},{8,10},{9,13},{10,... | collective-permute-start | bytes 786440 | tf_op jit(solution)/shard_map/ppermute | solution.py:86
  42.0 4.3 %collective-permute-done.8 = bf16[4,2,32,512]{3,2,1,0:T(8,128)(2,1)S(1)} collective-permute-done((bf16[4,2,32,512]{3,2,1,0:T(8,128)(2,1)S(1)}, bf16[4,2,32,512]{3,2,1,0:T(8,128)(2,1)S(1)}, u32[]{:S(2)}, u32[]{:S(2)}) %collective-permute-start.8) | collective-permute-done | bytes 262176 | tf_op jit(solution)/shard_map/ppermute | solution.py:86
  46.5 3.6 %collective-permute-done.7 = bf16[4,2,32,512]{3,2,1,0:T(8,128)(2,1)S(1)} collective-permute-done((bf16[4,2,32,512]{3,2,1,0:T(8,128)(2,1)S(1)}, bf16[4,2,32,512]{3,2,1,0:T(8,128)(2,1)S(1)}, u32[]{:S(2)}, u32[]{:S(2)}) %collective-permute-start.7) | collective-permute-done | bytes 262176 | tf_op jit(solution)/shard_map/ppermute | solution.py:86
  50.1 2.7 %collective-permute-done.9 = bf16[4,2,32,512]{3,2,1,0:T(8,128)(2,1)S(1)} collective-permute-done((bf16[4,2,32,512]{3,2,1,0:T(8,128)(2,1)S(1)}, bf16[4,2,32,512]{3,2,1,0:T(8,128)(2,1)S(1)}, u32[]{:S(2)}, u32[]{:S(2)}) %collective-permute-start.9) | collective-permute-done | bytes 262176 | tf_op jit(solution)/shard_map/ppermute | solution.py:86
  53.0 0.3 collective-permute-start.10
  53.3 1.5 %collective-permute-start.12 = (bf16[2,32,512]{2,1,0:T(8,128)(2,1)S(1)}, bf16[2,32,512]{2,1,0:T(8,128)(2,1)S(1)}, u32[]{:S(2)}, u32[]{:S(2)}) collective-permute-start(bf16[2,32,512]{2,1,0:T(8,128)(2,1)S(1)} %get-tuple-element.18), channel_id=1, source_target_pairs={{0,24},{1,25},{2,26},{3,27},{4,28},{5,29},{6,30},{7,31},{8,16},{9,... | collective-permute-start | bytes 196616 | tf_op jit(solution)/shard_map/ppermute | solution.py:86
  54.8 1.8 %collective-permute-start.11 = (bf16[2,32,512]{2,1,0:T(8,128)(2,1)S(1)}, bf16[2,32,512]{2,1,0:T(8,128)(2,1)S(1)}, u32[]{:S(2)}, u32[]{:S(2)}) collective-permute-start(bf16[2,32,512]{2,1,0:T(8,128)(2,1)S(1)} %get-tuple-element.19), channel_id=1, source_target_pairs={{0,16},{1,17},{2,18},{3,19},{4,20},{5,21},{6,22},{7,23},{8,24},{9,... | collective-permute-start | bytes 196616 | tf_op jit(solution)/shard_map/ppermute | solution.py:86
  56.5 1.8 %collective-permute-done.10 = bf16[2,32,512]{2,1,0:T(8,128)(2,1)S(1)} collective-permute-done((bf16[2,32,512]{2,1,0:T(8,128)(2,1)S(1)}, bf16[2,32,512]{2,1,0:T(8,128)(2,1)S(1)}, u32[]{:S(2)}, u32[]{:S(2)}) %collective-permute-start.10) | collective-permute-done | bytes 65568 | tf_op jit(solution)/shard_map/ppermute | solution.py:86
  58.3 1.1 %collective-permute-done.12 = bf16[2,32,512]{2,1,0:T(8,128)(2,1)S(1)} collective-permute-done((bf16[2,32,512]{2,1,0:T(8,128)(2,1)S(1)}, bf16[2,32,512]{2,1,0:T(8,128)(2,1)S(1)}, u32[]{:S(2)}, u32[]{:S(2)}) %collective-permute-start.12) | collective-permute-done | bytes 65568 | tf_op jit(solution)/shard_map/ppermute | solution.py:86
  59.4 2.3 %collective-permute-done.11 = bf16[2,32,512]{2,1,0:T(8,128)(2,1)S(1)} collective-permute-done((bf16[2,32,512]{2,1,0:T(8,128)(2,1)S(1)}, bf16[2,32,512]{2,1,0:T(8,128)(2,1)S(1)}, u32[]{:S(2)}, u32[]{:S(2)}) %collective-permute-start.11) | collective-permute-done | bytes 65568 | tf_op jit(solution)/shard_map/ppermute | solution.py:86
  61.7 0.7 %fusion.2 = f32[2,32,512]{2,1,0:T(8,128)} fusion(f32[4,2,32,512]{3,2,1,0:T(8,128)S(1)} %get-tuple-element.14, bf16[2,32,512]{2,1,0:T(8,128)(2,1)S(1)} %collective-permute-done.12, bf16[2,32,512]{2,1,0:T(8,128)(2,1)S(1)} %collective-permute-done.11, bf16[2,32,512]{2,1,0:T(8,128)(2,1)S(1)} %collective-permute-done.10), kind=kLoop, calls=%fused_computation.6 | loop fusion | flops 196608 | bytes 458752 | tf_op jit(solution)/shard_map/add | solution.py:124
  (27 shorter events, 0.7 us)
Async XLA Ops:
  0.0 28.1 %copy-start.4 = (s32[1,16,2]{1,2,0:T(2,128)S(1)}, s32[1,16,2]{1,2,0:T(2,128)}, u32[]{:S(2)}) copy-start(s32[1,16,2]{1,2,0:T(2,128)} %param.10) | copy-start | bytes 388
  0.0 30.2 %copy-start.3 = (s32[1,1,12]{2,1,0:T(1,128)S(1)}, s32[1,1,12]{2,1,0:T(1,128)}, u32[]{:S(2)}) copy-start(s32[1,1,12]{2,1,0:T(1,128)} %targets.1) | copy-start | bytes 148
  0.0 30.2 %copy-start.2 = (s32[1,1,12]{2,1,0:T(1,128)S(1)}, s32[1,1,12]{2,1,0:T(1,128)}, u32[]{:S(2)}) copy-start(s32[1,1,12]{2,1,0:T(1,128)} %pairs.1) | copy-start | bytes 148
  0.0 30.2 %copy-start = (bf16[1,4,512,512]{3,2,1,0:T(8,128)(2,1)S(1)}, bf16[1,4,512,512]{3,2,1,0:T(8,128)(2,1)}, u32[]{:S(2)}) copy-start(bf16[1,4,512,512]{3,2,1,0:T(8,128)(2,1)} %right.1) | copy-start | bytes 6291460
  1.0 7.7 %collective-permute-start.2 = (bf16[1,2,32,512]{3,2,1,0:T(8,128)(2,1)S(1)}, bf16[1,2,32,512]{3,2,1,0:T(8,128)(2,1)S(1)}, u32[]{:S(2)}, u32[]{:S(2)}) collective-permute-start(bf16[1,2,32,512]{3,2,1,0:T(8,128)(2,1)S(1)} %get-tuple-element.16), channel_id=1, source_target_pairs={{0,24},{1,25},{2,26},{3,27},{4,28},{5,29},{6,30},{7,31},{8,16},{9,... | collective-permute-start | bytes 196616 | tf_op jit(solution)/shard_map/ppermute | solution.py:86
  6.2 5.6 %collective-permute-start.1 = (bf16[1,2,32,512]{3,2,1,0:T(8,128)(2,1)S(1)}, bf16[1,2,32,512]{3,2,1,0:T(8,128)(2,1)S(1)}, u32[]{:S(2)}, u32[]{:S(2)}) collective-permute-start(bf16[1,2,32,512]{3,2,1,0:T(8,128)(2,1)S(1)} %get-tuple-element.16), channel_id=1, source_target_pairs={{0,16},{1,17},{2,18},{3,19},{4,20},{5,21},{6,22},{7,23},{8,24},{9,... | collective-permute-start | bytes 196616 | tf_op jit(solution)/shard_map/ppermute | solution.py:86
  6.2 5.6 %collective-permute-start = (bf16[1,2,32,512]{3,2,1,0:T(8,128)(2,1)S(1)}, bf16[1,2,32,512]{3,2,1,0:T(8,128)(2,1)S(1)}, u32[]{:S(2)}, u32[]{:S(2)}) collective-permute-start(bf16[1,2,32,512]{3,2,1,0:T(8,128)(2,1)S(1)} %get-tuple-element.16), channel_id=1, source_target_pairs={{0,8},{1,9},{2,10},{3,11},{4,12},{5,13},{6,14},{7,15},{8,0},{9,1},... | collective-permute-start | bytes 196616 | tf_op jit(solution)/shard_map/ppermute | solution.py:86
  11.8 9.1 %collective-permute-start.3 = (bf16[4,2,32,512]{3,2,1,0:T(8,128)(2,1)S(1)}, bf16[4,2,32,512]{3,2,1,0:T(8,128)(2,1)S(1)}, u32[]{:S(2)}, u32[]{:S(2)}) collective-permute-start(bf16[4,2,32,512]{3,2,1,0:T(8,128)(2,1)S(1)} %pad_maximum_fusion), channel_id=1, source_target_pairs={{0,2},{1,5},{2,0},{3,7},{4,6},{5,1},{6,4},{7,3},{8,10},{9,13},{10,... | collective-permute-start | bytes 786440 | tf_op jit(solution)/shard_map/ppermute | solution.py:86
  13.4 8.2 %collective-permute-start.4 = (bf16[4,2,32,512]{3,2,1,0:T(8,128)(2,1)S(1)}, bf16[4,2,32,512]{3,2,1,0:T(8,128)(2,1)S(1)}, u32[]{:S(2)}, u32[]{:S(2)}) collective-permute-start(bf16[4,2,32,512]{3,2,1,0:T(8,128)(2,1)S(1)} %pad_maximum_fusion), channel_id=1, source_target_pairs={{0,4},{1,3},{2,6},{3,1},{4,0},{5,7},{6,2},{7,5},{8,12},{9,11},{10,... | collective-permute-start | bytes 786440 | tf_op jit(solution)/shard_map/ppermute | solution.py:86
  20.9 6.4 %collective-permute-start.5 = (bf16[4,2,32,512]{3,2,1,0:T(8,128)(2,1)S(1)}, bf16[4,2,32,512]{3,2,1,0:T(8,128)(2,1)S(1)}, u32[]{:S(2)}, u32[]{:S(2)}) collective-permute-start(bf16[4,2,32,512]{3,2,1,0:T(8,128)(2,1)S(1)} %collective-permute-done.3), channel_id=1, source_target_pairs={{0,4},{1,3},{2,6},{3,1},{4,0},{5,7},{6,2},{7,5},{8,12},{9,11},{10,... | collective-permute-start | bytes 786440 | tf_op jit(solution)/shard_map/ppermute | solution.py:86
  27.3 2.9 %collective-permute-start.6 = (bf16[16,2,32,512]{3,2,1,0:T(8,128)(2,1)S(1)}, bf16[16,2,32,512]{3,2,1,0:T(8,128)(2,1)}, u32[]{:S(2)}, u32[]{:S(2)}) collective-permute-start(bf16[16,2,32,512]{3,2,1,0:T(8,128)(2,1)S(1)} %constant_dynamic-update-slice_fusion.mine), channel_id=1, source_target_pairs={{0,1},{1,0},{2,3},{3,2},{4,5},{5,4},{6,7},{7,6},{8,9},{9,8},{10,11... | collective-permute-start | bytes 3145736 | tf_op jit(solution)/shard_map/ppermute | solution.py:98
  30.2 1.2 %copy-start.1 = (bf16[1,2,512,512]{3,2,1,0:T(8,128)(2,1)S(1)}, bf16[1,2,512,512]{3,2,1,0:T(8,128)(2,1)}, u32[]{:S(2)}) copy-start(bf16[1,2,512,512]{3,2,1,0:T(8,128)(2,1)} %left.1) | copy-start | bytes 3145732
  39.9 6.4 %collective-permute-start.8 = (bf16[4,2,32,512]{3,2,1,0:T(8,128)(2,1)S(1)}, bf16[4,2,32,512]{3,2,1,0:T(8,128)(2,1)S(1)}, u32[]{:S(2)}, u32[]{:S(2)}) collective-permute-start(bf16[4,2,32,512]{3,2,1,0:T(8,128)(2,1)S(1)} %get-tuple-element.12), channel_id=1, source_target_pairs={{0,2},{1,5},{2,0},{3,7},{4,6},{5,1},{6,4},{7,3},{8,10},{9,13},{10,... | collective-permute-start | bytes 786440 | tf_op jit(solution)/shard_map/ppermute | solution.py:86
  40.0 10.1 %collective-permute-start.7 = (bf16[4,2,32,512]{3,2,1,0:T(8,128)(2,1)S(1)}, bf16[4,2,32,512]{3,2,1,0:T(8,128)(2,1)S(1)}, u32[]{:S(2)}, u32[]{:S(2)}) collective-permute-start(bf16[4,2,32,512]{3,2,1,0:T(8,128)(2,1)S(1)} %get-tuple-element.10), channel_id=1, source_target_pairs={{0,2},{1,5},{2,0},{3,7},{4,6},{5,1},{6,4},{7,3},{8,10},{9,13},{10,... | collective-permute-start | bytes 786440 | tf_op jit(solution)/shard_map/ppermute | solution.py:86
  46.4 6.4 %collective-permute-start.9 = (bf16[4,2,32,512]{3,2,1,0:T(8,128)(2,1)S(1)}, bf16[4,2,32,512]{3,2,1,0:T(8,128)(2,1)S(1)}, u32[]{:S(2)}, u32[]{:S(2)}) collective-permute-start(bf16[4,2,32,512]{3,2,1,0:T(8,128)(2,1)S(1)} %add_convert_fusion), channel_id=1, source_target_pairs={{0,4},{1,3},{2,6},{3,1},{4,0},{5,7},{6,2},{7,5},{8,12},{9,11},{10,... | collective-permute-start | bytes 786440 | tf_op jit(solution)/shard_map/ppermute | solution.py:86
  53.0 5.3 %collective-permute-start.10 = (bf16[2,32,512]{2,1,0:T(8,128)(2,1)S(1)}, bf16[2,32,512]{2,1,0:T(8,128)(2,1)S(1)}, u32[]{:S(2)}, u32[]{:S(2)}) collective-permute-start(bf16[2,32,512]{2,1,0:T(8,128)(2,1)S(1)} %get-tuple-element.17), channel_id=1, source_target_pairs={{0,8},{1,9},{2,10},{3,11},{4,12},{5,13},{6,14},{7,15},{8,0},{9,1},... | collective-permute-start | bytes 196616 | tf_op jit(solution)/shard_map/ppermute | solution.py:86
  53.3 6.1 %collective-permute-start.12 = (bf16[2,32,512]{2,1,0:T(8,128)(2,1)S(1)}, bf16[2,32,512]{2,1,0:T(8,128)(2,1)S(1)}, u32[]{:S(2)}, u32[]{:S(2)}) collective-permute-start(bf16[2,32,512]{2,1,0:T(8,128)(2,1)S(1)} %get-tuple-element.18), channel_id=1, source_target_pairs={{0,24},{1,25},{2,26},{3,27},{4,28},{5,29},{6,30},{7,31},{8,16},{9,... | collective-permute-start | bytes 196616 | tf_op jit(solution)/shard_map/ppermute | solution.py:86
  54.8 7.0 %collective-permute-start.11 = (bf16[2,32,512]{2,1,0:T(8,128)(2,1)S(1)}, bf16[2,32,512]{2,1,0:T(8,128)(2,1)S(1)}, u32[]{:S(2)}, u32[]{:S(2)}) collective-permute-start(bf16[2,32,512]{2,1,0:T(8,128)(2,1)S(1)} %get-tuple-element.19), channel_id=1, source_target_pairs={{0,16},{1,17},{2,18},{3,19},{4,20},{5,21},{6,22},{7,23},{8,24},{9,... | collective-permute-start | bytes 196616 | tf_op jit(solution)/shard_map/ppermute | solution.py:86

commit v2 on v1

v2 whole, which is shorter than its diff:
```python
import functools

import jax
import jax.numpy as jnp
from jax import lax
from jax.experimental import pallas as pl
from jax.experimental.pallas import tpu as pltpu
from jax.sharding import PartitionSpec as P

AXES = ("term", "sector")
BF16 = jnp.bfloat16
F32 = jnp.float32
VMEM = pl.BlockSpec(memory_space=pltpu.VMEM)
SMEM = pl.BlockSpec(memory_space=pltpu.SMEM)
VMEM_BYTES = 24 * 2**20
GROUPS = ((3,), (1,), (2, 0))


def block_rows(me, core, quarter, level, rows):
    near = jnp.where(core == 0, quarter, (0, 2, 1, 3)[quarter])
    owner = lax.bitwise_xor(me, near + 4 * level)
    return pl.ds(pl.multiple_of(owner * rows, rows), rows)


def prepare_kernel(rows, place, wanted, left, right, *refs):
    lefts, lasts = refs[:len(GROUPS)], refs[len(GROUPS):2 * len(GROUPS)]
    turned, sources, flipped, picked = refs[2 * len(GROUPS):]
    me, core = place[0], place[1]
    depth = left.shape[2] // (4 * rows)
    sources[0], sources[1] = me, core
    for j in range(wanted.shape[2]):
        sources[2 + j] = wanted[0, me, j]
    for a in range(left.shape[1]):
        for out, last, quarters in zip(lefts, lasts, GROUPS):
            used = out.shape[1]
            for i, quarter in enumerate(quarters):
                for level in range(depth):
                    window = block_rows(me, core, quarter, level, rows)
                    out[a, pl.ds((i * depth + level) * rows, rows), :] = left[0, a, window, :]
            flipped[:, :used] = out[a].T
            for level in range(depth):
                window = block_rows(me, core, 3, level, rows)
                picked[pl.ds(level * rows, rows), :used] = flipped[window, :used]
            last[a] = picked[:, :used].T
    for r in range(right.shape[1]):
        turned[r] = right[0, r].T


def early_kernel(sources, mine, other, *refs):
    lefts, sums, wave = refs[:len(GROUPS)], refs[len(GROUPS):2 * len(GROUPS)], refs[-1]
    half_sectors, rows = mine.shape[1], mine.shape[2]
    depth = mine.shape[0] // 3
    me, core = sources[0], sources[1]
    for j in range(wave.shape[0]):
        source = sources[2 + j]
        for level in range(depth):
            window = block_rows(me, core, 3, level, rows)
            wave[j, window, :] = jnp.zeros((rows, wave.shape[2]), wave.dtype)

        def unpack(blocks, from_core):
            for quarter in range(3):
                for level in range(depth):
                    block = blocks[quarter * depth + level, source % half_sectors]
                    wave[j, block_rows(me, from_core, quarter, level, rows), :] = block.astype(wave.dtype)

        @pl.when(source // half_sectors == core)
        def _():
            unpack(mine, core)

        @pl.when(source // half_sectors != core)
        def _():
            unpack(other, 1 - core)

    for left, out in zip(lefts, sums):
        for a in range(left.shape[0]):
            for j in range(wave.shape[0]):
                out[a * wave.shape[0] + j] = jnp.dot(
                    left[a].astype(BF16), wave[j].astype(BF16), preferred_element_type=F32
                )


def products(pairs, targets, live, early, left_last, wave_last, turned, outs, halves, total):
    ops_r, need = turned.shape[0], wave_last.shape[0]
    for a in range(left_last.shape[0]):
        for j in range(need):
            late = jnp.dot(left_last[a].astype(BF16), wave_last[j].astype(BF16), preferred_element_type=F32)
            halves[a * need + j] = (early[a * need + j] + late).astype(BF16)

    total[...] = jnp.zeros_like(total)
    for slot in range(pairs.shape[2]):
        code = pairs[0, 0, slot]
        target = jnp.where(slot < live[0, 0], targets[0, 0, slot], total.shape[0] - 1)
        total[target] += jnp.dot(halves[code // ops_r], turned[code % ops_r], preferred_element_type=F32)

    for i, out in enumerate(outs):
        depth, sec_dev, rows = out.shape[:3]
        for level in range(depth):
            for t in range(sec_dev):
                out[level, t] = total[t, pl.ds((i * depth + level) * rows, rows), :].astype(out.dtype)


def first_kernel(sources, pairs, targets, live, mine_last, other_last, early, left_last, turned,
                 wave_last, out, halves, total):
    depth, half_sectors, rows, size = mine_last.shape
    for j in range(wave_last.shape[0]):
        source = sources[2 + j]
        for owned, blocks in ((True, mine_last), (False, other_last)):
            @pl.when((source // half_sectors == sources[1]) == owned)
            def _(blocks=blocks):
                for level in range(depth):
                    block = blocks[level, source % half_sectors]
                    wave_last[j, pl.ds(level * rows, rows), :] = block.astype(wave_last.dtype)

    products(pairs, targets, live, early, left_last, wave_last, turned, [out], halves, total)


def next_kernel(pairs, targets, live, early, left_last, wave_last, turned, *refs):
    products(pairs, targets, live, early, left_last, wave_last, turned, refs[:-2], *refs[-2:])


def call(kernel, out_shapes, scratch_shapes, flops, *operands):
    def spec(array):
        return SMEM if jnp.issubdtype(array.dtype, jnp.integer) else VMEM

    return pl.pallas_call(
        kernel,
        out_shape=out_shapes,
        in_specs=[spec(operand) for operand in operands],
        out_specs=[spec(out) for out in out_shapes],
        scratch_shapes=scratch_shapes,
        compiler_params=pltpu.CompilerParams(vmem_limit_bytes=VMEM_BYTES),
        cost_estimate=pl.CostEstimate(flops=flops, bytes_accessed=2**20, transcendentals=0),
    )(*operands)


def on_device(terms, cores, wave_blocks, left_ops, right_ops, wanted, pairs, targets, live):
    sectors, rows, size = wave_blocks.shape
    me = lax.axis_index("term")
    core = lax.axis_index("sector") % 2
    depth = terms // 4
    sec_dev = sectors // cores
    ops_l, ops_r, need = left_ops.shape[1], right_ops.shape[1], wanted.shape[2]
    half = sectors // 2
    quarter = depth * rows
    shape = jax.ShapeDtypeStruct

    def swap(array, near, level=0):
        def partner(t, c):
            return t ^ (near[c % 2] + 4 * level)
        pairs_of = [(t * cores + c, partner(t, c) * cores + c) for t in range(terms) for c in range(cores)]
        return lax.ppermute(array, AXES, pairs_of)

    none, first, second = (0, 0), (1, 2), (2, 1)
    across = [(t * cores + c, t * cores + (c ^ 1)) for t in range(terms) for c in range(cores)]

    work_type = BF16 if rows % 16 == 0 else F32
    used = [len(group) * quarter for group in GROUPS]
    place = jnp.stack([me, core]).astype(jnp.int32)
    *prepared, sources = call(
        functools.partial(prepare_kernel, rows),
        [shape((ops_l, u, size), work_type) for u in used]
        + [shape((ops_l, u, quarter), work_type) for u in used]
        + [shape((ops_r, size, size), BF16), shape((2 + need,), jnp.int32)],
        [pltpu.VMEM((size, max(used)), work_type), pltpu.VMEM((quarter, max(used)), work_type)],
        size**3, place, wanted, left_ops.astype(work_type), right_ops,
    )

    own = lax.dynamic_slice_in_dim(wave_blocks, core * half, half, 0)[None]
    line = jnp.concatenate([own] + [swap(own, none, k) for k in range(1, depth)], 0)
    line, prepared, sources = lax.optimization_barrier((line, prepared, sources))
    lefts, lasts, turned = prepared[:len(GROUPS)], prepared[len(GROUPS):-1], prepared[-1]
    from_first = swap(line, first)
    from_second = swap(line, second)
    mine_last = swap(from_first, second)
    mine = jnp.concatenate([line, from_first, from_second], 0)
    other = lax.ppermute(mine, AXES, across)
    early = call(
        early_kernel,
        [shape((ops_l * need, u, size), F32) for u in used],
        [pltpu.VMEM((need, size, size), work_type)],
        8 * size**3, sources, mine, other, *lefts,
    )
    mine_last, early = lax.optimization_barrier((mine_last, early))
    other_last = lax.ppermute(mine_last, AXES, across)

    def sums(kernel, group, extra, kinds, *operands):
        return call(
            kernel, extra + [shape((depth, sec_dev, rows, size), kind) for kind in kinds],
            [pltpu.VMEM((ops_l * need, used[group], size), BF16), pltpu.VMEM((sec_dev + 1, used[group], size), F32)],
            24 * used[group] * size**2, *operands,
        )

    wave_last, far = sums(
        first_kernel, 0, [shape((need, quarter, size), work_type)], (BF16,),
        sources, pairs, targets, live, mine_last, other_last, early[0], lasts[0], turned,
    )
    far = swap(far, first)
    near, = sums(next_kernel, 1, [], (BF16,), pairs, targets, live, early[1], lasts[1], wave_last, turned)
    near = swap(near, first)
    passing, keep = sums(next_kernel, 2, [], (F32, F32), pairs, targets, live, early[2], lasts[2], wave_last, turned)

    passing = (passing + far.astype(F32)).astype(BF16)
    pass_rest = swap(passing[1:], second)
    line_rest = (keep[1:] + near[1:].astype(F32) + pass_rest.astype(F32)).astype(BF16)
    line_rest, pass_own = lax.optimization_barrier((line_rest, passing[0]))
    arrived = [swap(line_rest[k - 1], none, k) for k in range(1, depth)]
    pass_own = swap(pass_own, second)
    sigma = keep[0] + near[0].astype(F32) + pass_own.astype(F32)
    for part in arrived:
        sigma = sigma + part.astype(F32)
    return sigma


def solution(mesh):
    return jax.shard_map(
        functools.partial(on_device, mesh.shape["term"], mesh.shape["sector"]),
        mesh=mesh,
        in_specs=(
            P(None, "term", None),
            P("sector", "term", None, None),
            P("sector", "term", None, None),
            P("sector", None, None),
            P("sector", "term", None),
            P("sector", "term", None),
            P("sector", "term"),
        ),
        out_specs=P("sector", "term", None),
        check_vma=False,
    )
```

time: 63 us -> 55.5 us (0.88)
  waiting for transfers between devices: 34.5 us -> 19.4 us
  starting transfers between devices: 15.2 us -> 18.6 us
  Pallas kernels: 8.46 us -> 10.9 us
  local copies, waits for them, and re-layouts: 2.4 us -> 4.58 us
    ppermute x12 -> x13, waiting for transfers between devices: 32.6 us -> 17.3 us  [swap(): return lax.ppermute(array, AXES, pairs_of)]
    ppermute x12 -> x13, starting transfers between devices: 15.2 us -> 18.5 us  [swap(): return lax.ppermute(array, AXES, pairs_of)]
    pallas_call x1 -> x5, Pallas kernels: 8.46 us -> 10.9 us  [call(): pl.pallas_call(kernel, out_shape=out_shapes, in_specs=[spec(operand) for...]
    unnamed x17 -> x13, local copies, waits for them, and re-layouts: 2.37 us -> 4.52 us
    ppermute x0 -> x1, waiting for transfers between devices: none -> 0.88 us  [on_device(): other_last = lax.ppermute(mine_last, AXES, across)]
    ppermute x1, waiting for transfers between devices: 1.96 us -> 1.18 us  [on_device(): other = lax.ppermute(mine, AXES, across)]
  transfers between devices with their start and end apart: 13 -> 15, of which waited for: 11 -> 9; matrix products, arithmetic and copies ran while one was open for 0% -> 2% of each run, Pallas kernels for 0% -> 16%
where the time goes in v2:
time: 55.5 us; the launch traced here: 55.3 us
  waiting for transfers between devices  19.4 us (35%)
  starting transfers between devices  18.6 us (34%)
  Pallas kernels  10.9 us (20%)
  local copies, waits for them, and re-layouts  4.58 us (8%)
  other arithmetic  0.98 us (2%)
  between operations  0.81 us (1%)
    ppermute x13, starting transfers between devices, swap(): return lax.ppermute(array, AXES, pairs_of)  18.5 us
    ppermute x13, waiting for transfers between devices, swap(): return lax.ppermute(array, AXES, pairs_of)  17.3 us
    pallas_call x5, Pallas kernels, call(): pl.pallas_call(kernel, out_shape=out_shapes, in_specs=[spec(operand) for...  10.9 us
    unnamed x13, local copies, waits for them, and re-layouts  4.52 us
    ppermute x1, waiting for transfers between devices, on_device(): other = lax.ppermute(mine, AXES, across)  1.18 us
  transfers between devices with their start and end apart: 15, of which 9 were waited for; matrix products, arithmetic and copies ran while one was open for 2% of the time, Pallas kernels for 16%

profile of v2, /device:TPU:0, one launch (start us, length us, event | category | flops | bytes accessed | tf_op | source)
XLA Modules:
  0.0 55.3 jit_solution(3568302892840764206)
XLA Ops:
  0.0 0.9 %copy-done = bf16[4,32,512]{2,1,0:T(8,128)(2,1)S(1)} copy-done((bf16[4,32,512]{2,1,0:T(8,128)(2,1)S(1)}, bf16[4,32,512]{2,1,0:T(8,128)(2,1)}, u32[]{:S(2)}) %copy-start) | copy-done | bytes 131096
  0.9 3.0 %collective-permute-start = (bf16[1,2,32,512]{3,2,1,0:T(8,128)(2,1)S(1)}, bf16[1,2,32,512]{3,2,1,0:T(8,128)(2,1)S(1)}, u32[]{:S(2)}, u32[]{:S(2)}) collective-permute-start(bf16[1,2,32,512]{3,2,1,0:T(8,128)(2,1)S(1)} %dynamic-slice_bitcast_fusion), channel_id=1, source_target_pairs={{0,8},{1,9},{2,10},{3,11},{4,12},{5,13},{6,14},{7,15},{8,0},{9,1},... | collective-permute-start | bytes 196616 | tf_op jit(solution)/shard_map/ppermute | solution.py:151
  3.9 2.6 %collective-permute-start.1 = (bf16[1,2,32,512]{3,2,1,0:T(8,128)(2,1)S(1)}, bf16[1,2,32,512]{3,2,1,0:T(8,128)(2,1)S(1)}, u32[]{:S(2)}, u32[]{:S(2)}) collective-permute-start(bf16[1,2,32,512]{3,2,1,0:T(8,128)(2,1)S(1)} %dynamic-slice_bitcast_fusion), channel_id=1, source_target_pairs={{0,16},{1,17},{2,18},{3,19},{4,20},{5,21},{6,22},{7,23},{8,24},{9,... | collective-permute-start | bytes 196616 | tf_op jit(solution)/shard_map/ppermute | solution.py:151
  7.4 1.6 %copy-done.1 = bf16[1,4,512,512]{3,2,1,0:T(8,128)(2,1)S(1)} copy-done((bf16[1,4,512,512]{3,2,1,0:T(8,128)(2,1)S(1)}, bf16[1,4,512,512]{3,2,1,0:T(8,128)(2,1)}, u32[]{:S(2)}) %copy-start.1) | copy-done | bytes 2097176
  9.0 1.2 %copy-done.2 = bf16[1,2,512,512]{3,2,1,0:T(8,128)(2,1)S(1)} copy-done((bf16[1,2,512,512]{3,2,1,0:T(8,128)(2,1)S(1)}, bf16[1,2,512,512]{3,2,1,0:T(8,128)(2,1)}, u32[]{:S(2)}) %copy-start.2) | copy-done | bytes 1048600
  10.2 2.0 %shard_map.73 = (bf16[2,128,512]{2,1,0:T(8,128)(2,1)S(1)}, bf16[2,128,512]{2,1,0:T(8,128)(2,1)S(1)}, bf16[2,256,512]{2,1,0:T(8,128)(2,1)S(1)}, bf16[2,128,128]{2...) custom-call(s32[2]{0:T(128)S(1)} %pad_add_fusion.place, ...), custom_call_target="tpu_custom_call" | custom-call | flops 134217728 | bytes 1048576 | tf_op jit(solution)/shard_map/pallas_call | solution.py:125
  12.6 1.6 %collective-permute-start.3 = (bf16[4,2,32,512]{3,2,1,0:T(8,128)(2,1)S(1)}, bf16[4,2,32,512]{3,2,1,0:T(8,128)(2,1)S(1)}, u32[]{:S(2)}, u32[]{:S(2)}) collective-permute-start(bf16[4,2,32,512]{3,2,1,0:T(8,128)(2,1)S(1)} %pad_maximum_fusion), channel_id=1, source_target_pairs={{0,2},{1,5},{2,0},{3,7},{4,6},{5,1},{6,4},{7,3},{8,10},{9,13},{10,... | collective-permute-start | bytes 786440 | tf_op jit(solution)/shard_map/ppermute | solution.py:151
  14.2 1.5 %collective-permute-start.5 = (bf16[4,2,32,512]{3,2,1,0:T(8,128)(2,1)S(1)}, bf16[4,2,32,512]{3,2,1,0:T(8,128)(2,1)S(1)}, u32[]{:S(2)}, u32[]{:S(2)}) collective-permute-start(bf16[4,2,32,512]{3,2,1,0:T(8,128)(2,1)S(1)} %pad_maximum_fusion), channel_id=1, source_target_pairs={{0,4},{1,3},{2,6},{3,1},{4,0},{5,7},{6,2},{7,5},{8,12},{9,11},{10,... | collective-permute-start | bytes 786440 | tf_op jit(solution)/shard_map/ppermute | solution.py:151
  15.7 5.3 %collective-permute-done.3 = bf16[4,2,32,512]{3,2,1,0:T(8,128)(2,1)S(1)} collective-permute-done((bf16[4,2,32,512]{3,2,1,0:T(8,128)(2,1)S(1)}, bf16[4,2,32,512]{3,2,1,0:T(8,128)(2,1)S(1)}, u32[]{:S(2)}, u32[]{:S(2)}) %collective-permute-start.3) | collective-permute-done | bytes 262176 | tf_op jit(solution)/shard_map/ppermute | solution.py:151
  21.2 1.1 %collective-permute-start.4 = (bf16[4,2,32,512]{3,2,1,0:T(8,128)(2,1)S(1)}, bf16[4,2,32,512]{3,2,1,0:T(8,128)(2,1)S(1)}, u32[]{:S(2)}, u32[]{:S(2)}) collective-permute-start(bf16[4,2,32,512]{3,2,1,0:T(8,128)(2,1)S(1)} %collective-permute-done.3), channel_id=1, source_target_pairs={{0,4},{1,3},{2,6},{3,1},{4,0},{5,7},{6,2},{7,5},{8,12},{9,11},{10,... | collective-permute-start | bytes 786440 | tf_op jit(solution)/shard_map/ppermute | solution.py:151
  22.3 1.2 %collective-permute-done.6.other = bf16[12,2,32,512]{3,2,1,0:T(8,128)(2,1)S(1)} collective-permute-done((bf16[12,2,32,512]{3,2,1,0:T(8,128)(2,1)S(1)}, bf16[12,2,32,512]{3,2,1,0:T(8,128)(2,1)S(1)}, u32[]{:S(2)}, u32[]{:S(2)}) %collective-permute-start.6) | collective-permute-done | bytes 786464 | tf_op jit(solution)/shard_map/ppermute | solution.py:176
  23.5 1.9 %shard_map.74 = (f32[4,128,512]{2,1,0:T(8,128)S(1)}, f32[4,128,512]{2,1,0:T(8,128)S(1)}, f32[4,256,512]{2,1,0:T(8,128)S(1)}) custom-call(s32[4]{0:T(128)S(1)} %get-tuple-element.44.sources, bf16[12,2,32,512]{3,2,1,0:T(8,128)(2,1)S(1)} %constant_dynamic-update-slice_fusion.mine, bf16[12,2,32,512]{3,2,1,0:T(8,128)(2,1)S(1)} %collective-permute-done.6.other, ...), custom_call_target="tpu_custom_call" | custom-call | flops 1073741824 | bytes 1048576 | tf_op jit(solution)/shard_map/pallas_call | solution.py:125
  25.4 2.2 %collective-permute-done.4.mine_last = bf16[4,2,32,512]{3,2,1,0:T(8,128)(2,1)S(1)} collective-permute-done((bf16[4,2,32,512]{3,2,1,0:T(8,128)(2,1)S(1)}, bf16[4,2,32,512]{3,2,1,0:T(8,128)(2,1)S(1)}, u32[]{:S(2)}, u32[]{:S(2)}) %collective-permute-start.4) | collective-permute-done | bytes 262176 | tf_op jit(solution)/shard_map/ppermute | solution.py:151
  29.2 2.0 %shard_map.75 = (bf16[2,128,512]{2,1,0:T(8,128)(2,1)S(1)}, bf16[4,2,32,512]{3,2,1,0:T(8,128)(2,1)S(1)}) custom-call(s32[4]{0:T(128)S(1)} %get-tuple-element.44.sources, s32[1,1,12]{2,1,0:T(1,128)S(1)} %copy-done.3, s32[1,1,12]{2,1,0:T(1,128)S(1)} %copy-done.4, s32[1,1]{1,0:T(1,128)S(6)} %copy.11.live, ...), custom_call_target="tpu_custom_call" | custom-call | flops 805306368 | bytes 1048576 | tf_op jit(solution)/shard_map/pallas_call | solution.py:125
  31.2 1.6 %collective-permute-start.9 = (bf16[4,2,32,512]{3,2,1,0:T(8,128)(2,1)S(1)}, bf16[4,2,32,512]{3,2,1,0:T(8,128)(2,1)S(1)}, u32[]{:S(2)}, u32[]{:S(2)}) collective-permute-start(bf16[4,2,32,512]{3,2,1,0:T(8,128)(2,1)S(1)} %get-tuple-element.62), channel_id=1, source_target_pairs={{0,2},{1,5},{2,0},{3,7},{4,6},{5,1},{6,4},{7,3},{8,10},{9,13},{10,... | collective-permute-start | bytes 786440 | tf_op jit(solution)/shard_map/ppermute | solution.py:151
  32.8 2.0 %shard_map.77 = bf16[4,2,32,512]{3,2,1,0:T(8,128)(2,1)S(1)} custom-call(s32[1,1,12]{2,1,0:T(1,128)S(1)} %copy-done.3, s32[1,1,12]{2,1,0:T(1,128)S(1)} %copy-done.4, s32[1,1]{1,0:T(1,128)S(6)} %copy.11.live, f32[4,128,512]{2,1,0:T(8,128)S(1)} %get-tuple-element.59.early, bf16[2,128,128]{2,1,0:T(8,128)(2,1)S(1)} %get-tuple-element.60.left_last, ...), custom_call_target="tpu_custom_call" | custom-call | flops 805306368 | bytes 1048576 | tf_op jit(solution)/shard_map/pallas_call | solution.py:125
  35.4 3.0 %shard_map.76 = (f32[4,2,32,512]{3,2,1,0:T(8,128)S(1)}, f32[4,2,32,512]{3,2,1,0:T(8,128)S(1)}) custom-call(s32[1,1,12]{2,1,0:T(1,128)S(1)} %copy-done.3, s32[1,1,12]{2,1,0:T(1,128)S(1)} %copy-done.4, s32[1,1]{1,0:T(1,128)S(6)} %copy.11.live, f32[4,256,512]{2,1,0:T(8,128)S(1)} %get-tuple-element.51.early, ...), custom_call_target="tpu_custom_call" | custom-call | flops 1610612736 | bytes 1048576 | tf_op jit(solution)/shard_map/pallas_call | solution.py:125
  38.5 1.1 %collective-permute-start.10 = (bf16[3,2,32,512]{3,2,1,0:T(8,128)(2,1)S(1)}, bf16[3,2,32,512]{3,2,1,0:T(8,128)(2,1)S(1)}, u32[]{:S(2)}, u32[]{:S(2)}) collective-permute-start(bf16[3,2,32,512]{3,2,1,0:T(8,128)(2,1)S(1)} %slice.38), channel_id=1, source_target_pairs={{0,4},{1,3},{2,6},{3,1},{4,0},{5,7},{6,2},{7,5},{8,12},{9,11},{10,... | collective-permute-start | bytes 589832 | tf_op jit(solution)/shard_map/ppermute | solution.py:151
  39.6 2.0 %collective-permute-done.8 = bf16[4,2,32,512]{3,2,1,0:T(8,128)(2,1)S(1)} collective-permute-done((bf16[4,2,32,512]{3,2,1,0:T(8,128)(2,1)S(1)}, bf16[4,2,32,512]{3,2,1,0:T(8,128)(2,1)S(1)}, u32[]{:S(2)}, u32[]{:S(2)}) %collective-permute-start.8) | collective-permute-done | bytes 262176 | tf_op jit(solution)/shard_map/ppermute | solution.py:151
  41.6 2.6 %collective-permute-done.10 = bf16[3,2,32,512]{3,2,1,0:T(8,128)(2,1)S(1)} collective-permute-done((bf16[3,2,32,512]{3,2,1,0:T(8,128)(2,1)S(1)}, bf16[3,2,32,512]{3,2,1,0:T(8,128)(2,1)S(1)}, u32[]{:S(2)}, u32[]{:S(2)}) %collective-permute-start.10) | collective-permute-done | bytes 196640 | tf_op jit(solution)/shard_map/ppermute | solution.py:151
  45.0 3.5 %collective-permute-start.13 = (bf16[2,32,512]{2,1,0:T(8,128)(2,1)S(1)}, bf16[2,32,512]{2,1,0:T(8,128)(2,1)S(1)}, u32[]{:S(2)}, u32[]{:S(2)}) collective-permute-start(bf16[2,32,512]{2,1,0:T(8,128)(2,1)S(1)} %get-tuple-element.67), channel_id=1, source_target_pairs={{0,16},{1,17},{2,18},{3,19},{4,20},{5,21},{6,22},{7,23},{8,24},{9,... | collective-permute-start | bytes 196616 | tf_op jit(solution)/shard_map/ppermute | solution.py:151
  48.8 1.0 %collective-permute-start.11 = (bf16[2,32,512]{2,1,0:T(8,128)(2,1)S(1)}, bf16[2,32,512]{2,1,0:T(8,128)(2,1)S(1)}, u32[]{:S(2)}, u32[]{:S(2)}) collective-permute-start(bf16[2,32,512]{2,1,0:T(8,128)(2,1)S(1)} %slice_bitcast_fusion), channel_id=1, source_target_pairs={{0,4},{1,3},{2,6},{3,1},{4,0},{5,7},{6,2},{7,5},{8,12},{9,11},{10,... | collective-permute-start | bytes 196616 | tf_op jit(solution)/shard_map/ppermute | solution.py:151
  49.8 2.7 %collective-permute-done.13 = bf16[2,32,512]{2,1,0:T(8,128)(2,1)S(1)} collective-permute-done((bf16[2,32,512]{2,1,0:T(8,128)(2,1)S(1)}, bf16[2,32,512]{2,1,0:T(8,128)(2,1)S(1)}, u32[]{:S(2)}, u32[]{:S(2)}) %collective-permute-start.13) | collective-permute-done | bytes 65568 | tf_op jit(solution)/shard_map/ppermute | solution.py:151
  52.5 2.1 %collective-permute-done.14 = bf16[2,32,512]{2,1,0:T(8,128)(2,1)S(1)} collective-permute-done((bf16[2,32,512]{2,1,0:T(8,128)(2,1)S(1)}, bf16[2,32,512]{2,1,0:T(8,128)(2,1)S(1)}, u32[]{:S(2)}, u32[]{:S(2)}) %collective-permute-start.14) | collective-permute-done | bytes 65568 | tf_op jit(solution)/shard_map/ppermute | solution.py:151
  (34 shorter events, 4.8 us)
Async XLA Ops:
  0.0 0.9 %copy-start = (bf16[4,32,512]{2,1,0:T(8,128)(2,1)S(1)}, bf16[4,32,512]{2,1,0:T(8,128)(2,1)}, u32[]{:S(2)}) copy-start(bf16[4,32,512]{2,1,0:T(8,128)(2,1)} %param.7) | copy-start | bytes 393220
  0.9 11.3 %collective-permute-start = (bf16[1,2,32,512]{3,2,1,0:T(8,128)(2,1)S(1)}, bf16[1,2,32,512]{3,2,1,0:T(8,128)(2,1)S(1)}, u32[]{:S(2)}, u32[]{:S(2)}) collective-permute-start(bf16[1,2,32,512]{3,2,1,0:T(8,128)(2,1)S(1)} %dynamic-slice_bitcast_fusion), channel_id=1, source_target_pairs={{0,8},{1,9},{2,10},{3,11},{4,12},{5,13},{6,14},{7,15},{8,0},{9,1},... | collective-permute-start | bytes 196616 | tf_op jit(solution)/shard_map/ppermute | solution.py:151
  3.9 8.2 %collective-permute-start.1 = (bf16[1,2,32,512]{3,2,1,0:T(8,128)(2,1)S(1)}, bf16[1,2,32,512]{3,2,1,0:T(8,128)(2,1)S(1)}, u32[]{:S(2)}, u32[]{:S(2)}) collective-permute-start(bf16[1,2,32,512]{3,2,1,0:T(8,128)(2,1)S(1)} %dynamic-slice_bitcast_fusion), channel_id=1, source_target_pairs={{0,16},{1,17},{2,18},{3,19},{4,20},{5,21},{6,22},{7,23},{8,24},{9,... | collective-permute-start | bytes 196616 | tf_op jit(solution)/shard_map/ppermute | solution.py:151
  6.5 6.1 %collective-permute-start.2 = (bf16[1,2,32,512]{3,2,1,0:T(8,128)(2,1)S(1)}, bf16[1,2,32,512]{3,2,1,0:T(8,128)(2,1)S(1)}, u32[]{:S(2)}, u32[]{:S(2)}) collective-permute-start(bf16[1,2,32,512]{3,2,1,0:T(8,128)(2,1)S(1)} %dynamic-slice_bitcast_fusion), channel_id=1, source_target_pairs={{0,24},{1,25},{2,26},{3,27},{4,28},{5,29},{6,30},{7,31},{8,16},{9,... | collective-permute-start | bytes 196616 | tf_op jit(solution)/shard_map/ppermute | solution.py:151
  7.4 1.6 %copy-start.1 = (bf16[1,4,512,512]{3,2,1,0:T(8,128)(2,1)S(1)}, bf16[1,4,512,512]{3,2,1,0:T(8,128)(2,1)}, u32[]{:S(2)}) copy-start(bf16[1,4,512,512]{3,2,1,0:T(8,128)(2,1)} %right.1) | copy-start | bytes 6291460
  9.0 1.2 %copy-start.2 = (bf16[1,2,512,512]{3,2,1,0:T(8,128)(2,1)S(1)}, bf16[1,2,512,512]{3,2,1,0:T(8,128)(2,1)}, u32[]{:S(2)}) copy-start(bf16[1,2,512,512]{3,2,1,0:T(8,128)(2,1)} %left.1) | copy-start | bytes 3145732
  12.6 8.4 %collective-permute-start.3 = (bf16[4,2,32,512]{3,2,1,0:T(8,128)(2,1)S(1)}, bf16[4,2,32,512]{3,2,1,0:T(8,128)(2,1)S(1)}, u32[]{:S(2)}, u32[]{:S(2)}) collective-permute-start(bf16[4,2,32,512]{3,2,1,0:T(8,128)(2,1)S(1)} %pad_maximum_fusion), channel_id=1, source_target_pairs={{0,2},{1,5},{2,0},{3,7},{4,6},{5,1},{6,4},{7,3},{8,10},{9,13},{10,... | collective-permute-start | bytes 786440 | tf_op jit(solution)/shard_map/ppermute | solution.py:151
  14.2 6.9 %collective-permute-start.5 = (bf16[4,2,32,512]{3,2,1,0:T(8,128)(2,1)S(1)}, bf16[4,2,32,512]{3,2,1,0:T(8,128)(2,1)S(1)}, u32[]{:S(2)}, u32[]{:S(2)}) collective-permute-start(bf16[4,2,32,512]{3,2,1,0:T(8,128)(2,1)S(1)} %pad_maximum_fusion), channel_id=1, source_target_pairs={{0,4},{1,3},{2,6},{3,1},{4,0},{5,7},{6,2},{7,5},{8,12},{9,11},{10,... | collective-permute-start | bytes 786440 | tf_op jit(solution)/shard_map/ppermute | solution.py:151
  21.1 8.1 %copy-start.3 = (s32[1,1,12]{2,1,0:T(1,128)S(1)}, s32[1,1,12]{2,1,0:T(1,128)}, u32[]{:S(2)}) copy-start(s32[1,1,12]{2,1,0:T(1,128)} %pairs.5) | copy-start | bytes 148
  21.1 8.1 %copy-start.4 = (s32[1,1,12]{2,1,0:T(1,128)S(1)}, s32[1,1,12]{2,1,0:T(1,128)}, u32[]{:S(2)}) copy-start(s32[1,1,12]{2,1,0:T(1,128)} %targets.5) | copy-start | bytes 148
  21.1 2.4 %collective-permute-start.6 = (bf16[12,2,32,512]{3,2,1,0:T(8,128)(2,1)S(1)}, bf16[12,2,32,512]{3,2,1,0:T(8,128)(2,1)S(1)}, u32[]{:S(2)}, u32[]{:S(2)}) collective-permute-start(bf16[12,2,32,512]{3,2,1,0:T(8,128)(2,1)S(1)} %constant_dynamic-update-slice_fusion.mine), channel_id=1, source_target_pairs={{0,1},{1,0},{2,3},{3,2},{4,5},{5,4},{6,7},{7,6},{8,9},{9,8},{10,11... | collective-permute-start | bytes 2359304 | tf_op jit(solution)/shard_map/ppermute | solution.py:176
  21.2 6.4 %collective-permute-start.4 = (bf16[4,2,32,512]{3,2,1,0:T(8,128)(2,1)S(1)}, bf16[4,2,32,512]{3,2,1,0:T(8,128)(2,1)S(1)}, u32[]{:S(2)}, u32[]{:S(2)}) collective-permute-start(bf16[4,2,32,512]{3,2,1,0:T(8,128)(2,1)S(1)} %collective-permute-done.3), channel_id=1, source_target_pairs={{0,4},{1,3},{2,6},{3,1},{4,0},{5,7},{6,2},{7,5},{8,12},{9,11},{10,... | collective-permute-start | bytes 786440 | tf_op jit(solution)/shard_map/ppermute | solution.py:151
  27.6 1.5 %collective-permute-start.7 = (bf16[4,2,32,512]{3,2,1,0:T(8,128)(2,1)S(1)}, bf16[4,2,32,512]{3,2,1,0:T(8,128)(2,1)S(1)}, u32[]{:S(2)}, u32[]{:S(2)}) collective-permute-start(bf16[4,2,32,512]{3,2,1,0:T(8,128)(2,1)S(1)} %collective-permute-done.4.mine_last), channel_id=1, source_target_pairs={{0,1},{1,0},{2,3},{3,2},{4,5},{5,4},{6,7},{7,6},{8,9},{9,8},{10,11... | collective-permute-start | bytes 786440 | tf_op jit(solution)/shard_map/ppermute | solution.py:184
  31.2 7.1 %collective-permute-start.9 = (bf16[4,2,32,512]{3,2,1,0:T(8,128)(2,1)S(1)}, bf16[4,2,32,512]{3,2,1,0:T(8,128)(2,1)S(1)}, u32[]{:S(2)}, u32[]{:S(2)}) collective-permute-start(bf16[4,2,32,512]{3,2,1,0:T(8,128)(2,1)S(1)} %get-tuple-element.62), channel_id=1, source_target_pairs={{0,2},{1,5},{2,0},{3,7},{4,6},{5,1},{6,4},{7,3},{8,10},{9,13},{10,... | collective-permute-start | bytes 786440 | tf_op jit(solution)/shard_map/ppermute | solution.py:151
  34.8 6.9 %collective-permute-start.8 = (bf16[4,2,32,512]{3,2,1,0:T(8,128)(2,1)S(1)}, bf16[4,2,32,512]{3,2,1,0:T(8,128)(2,1)S(1)}, u32[]{:S(2)}, u32[]{:S(2)}) collective-permute-start(bf16[4,2,32,512]{3,2,1,0:T(8,128)(2,1)S(1)} %shard_map.77), channel_id=1, source_target_pairs={{0,2},{1,5},{2,0},{3,7},{4,6},{5,1},{6,4},{7,3},{8,10},{9,13},{10,... | collective-permute-start | bytes 786440 | tf_op jit(solution)/shard_map/ppermute | solution.py:151
  38.5 5.7 %collective-permute-start.10 = (bf16[3,2,32,512]{3,2,1,0:T(8,128)(2,1)S(1)}, bf16[3,2,32,512]{3,2,1,0:T(8,128)(2,1)S(1)}, u32[]{:S(2)}, u32[]{:S(2)}) collective-permute-start(bf16[3,2,32,512]{3,2,1,0:T(8,128)(2,1)S(1)} %slice.38), channel_id=1, source_target_pairs={{0,4},{1,3},{2,6},{3,1},{4,0},{5,7},{6,2},{7,5},{8,12},{9,11},{10,... | collective-permute-start | bytes 589832 | tf_op jit(solution)/shard_map/ppermute | solution.py:151
  44.3 5.5 %collective-permute-start.12 = (bf16[2,32,512]{2,1,0:T(8,128)(2,1)S(1)}, bf16[2,32,512]{2,1,0:T(8,128)(2,1)S(1)}, u32[]{:S(2)}, u32[]{:S(2)}) collective-permute-start(bf16[2,32,512]{2,1,0:T(8,128)(2,1)S(1)} %get-tuple-element.65), channel_id=1, source_target_pairs={{0,8},{1,9},{2,10},{3,11},{4,12},{5,13},{6,14},{7,15},{8,0},{9,1},... | collective-permute-start | bytes 196616 | tf_op jit(solution)/shard_map/ppermute | solution.py:151
  45.0 7.5 %collective-permute-start.13 = (bf16[2,32,512]{2,1,0:T(8,128)(2,1)S(1)}, bf16[2,32,512]{2,1,0:T(8,128)(2,1)S(1)}, u32[]{:S(2)}, u32[]{:S(2)}) collective-permute-start(bf16[2,32,512]{2,1,0:T(8,128)(2,1)S(1)} %get-tuple-element.67), channel_id=1, source_target_pairs={{0,16},{1,17},{2,18},{3,19},{4,20},{5,21},{6,22},{7,23},{8,24},{9,... | collective-permute-start | bytes 196616 | tf_op jit(solution)/shard_map/ppermute | solution.py:151
  48.5 6.1 %collective-permute-start.14 = (bf16[2,32,512]{2,1,0:T(8,128)(2,1)S(1)}, bf16[2,32,512]{2,1,0:T(8,128)(2,1)S(1)}, u32[]{:S(2)}, u32[]{:S(2)}) collective-permute-start(bf16[2,32,512]{2,1,0:T(8,128)(2,1)S(1)} %get-tuple-element.66), channel_id=1, source_target_pairs={{0,24},{1,25},{2,26},{3,27},{4,28},{5,29},{6,30},{7,31},{8,16},{9,... | collective-permute-start | bytes 196616 | tf_op jit(solution)/shard_map/ppermute | solution.py:151
  48.8 5.8 %collective-permute-start.11 = (bf16[2,32,512]{2,1,0:T(8,128)(2,1)S(1)}, bf16[2,32,512]{2,1,0:T(8,128)(2,1)S(1)}, u32[]{:S(2)}, u32[]{:S(2)}) collective-permute-start(bf16[2,32,512]{2,1,0:T(8,128)(2,1)S(1)} %slice_bitcast_fusion), channel_id=1, source_target_pairs={{0,4},{1,3},{2,6},{3,1},{4,0},{5,7},{6,2},{7,5},{8,12},{9,11},{10,... | collective-permute-start | bytes 196616 | tf_op jit(solution)/shard_map/ppermute | solution.py:151

commit v3 on v2

--- a/solution.py
+++ b/solution.py
@@ -141,6 +141,7 @@
     sec_dev = sectors // cores
     ops_l, ops_r, need = left_ops.shape[1], right_ops.shape[1], wanted.shape[2]
     half = sectors // 2
+    far_first = sorted(range(1, depth), key=lambda k: (k ^ (depth - 1)) & -2)
     quarter = depth * rows
     shape = jax.ShapeDtypeStruct
 
@@ -166,7 +167,8 @@
     )
 
     own = lax.dynamic_slice_in_dim(wave_blocks, core * half, half, 0)[None]
-    line = jnp.concatenate([own] + [swap(own, none, k) for k in range(1, depth)], 0)
+    by_level = {k: swap(own, none, k) for k in far_first}
+    line = jnp.concatenate([own] + [by_level[k] for k in range(1, depth)], 0)
     line, prepared, sources = lax.optimization_barrier((line, prepared, sources))
     lefts, lasts, turned = prepared[:len(GROUPS)], prepared[len(GROUPS):-1], prepared[-1]
     from_first = swap(line, first)
@@ -203,7 +205,7 @@
     pass_rest = swap(passing[1:], second)
     line_rest = (keep[1:] + near[1:].astype(F32) + pass_rest.astype(F32)).astype(BF16)
     line_rest, pass_own = lax.optimization_barrier((line_rest, passing[0]))
-    arrived = [swap(line_rest[k - 1], none, k) for k in range(1, depth)]
+    arrived = [swap(line_rest[k - 1], none, k) for k in far_first]
     pass_own = swap(pass_own, second)
     sigma = keep[0] + near[0].astype(F32) + pass_own.astype(F32)
     for part in arrived:

time: 55.5 us -> 53.8 us (0.969)
  waiting for transfers between devices: 19.4 us -> 18.1 us
    ppermute x13, waiting for transfers between devices: 17.3 us -> 16.1 us  [swap(): return lax.ppermute(array, AXES, pairs_of)]
  transfers between devices with their start and end apart: 15 -> 15, of which waited for: 9 -> 10; matrix products, arithmetic and copies ran while one was open for 2% -> 2% of each run, Pallas kernels for 16% -> 17%
where the time goes in v3:
time: 53.8 us; the launch traced here: 53.6 us
  starting transfers between devices  18.2 us (34%)
  waiting for transfers between devices  18.1 us (34%)
  Pallas kernels  10.9 us (20%)
  local copies, waits for them, and re-layouts  4.58 us (9%)
  other arithmetic  0.98 us (2%)
  between operations  0.81 us (2%)
    ppermute x13, starting transfers between devices, swap(): return lax.ppermute(array, AXES, pairs_of)  18.1 us
    ppermute x13, waiting for transfers between devices, swap(): return lax.ppermute(array, AXES, pairs_of)  16.1 us
    pallas_call x5, Pallas kernels, call(): pl.pallas_call(kernel, out_shape=out_shapes, in_specs=[spec(operand) for...  10.9 us
    unnamed x13, local copies, waits for them, and re-layouts  4.52 us
    ppermute x1, waiting for transfers between devices, on_device(): other = lax.ppermute(mine, AXES, across)  1.18 us
  transfers between devices with their start and end apart: 15, of which 10 were waited for; matrix products, arithmetic and copies ran while one was open for 2% of the time, Pallas kernels for 17%

profile of v3, /device:TPU:0, one launch (start us, length us, event | category | flops | bytes accessed | tf_op | source)
XLA Modules:
  0.0 53.6 jit_solution(16871784489915167927)
XLA Ops:
  0.0 0.9 %copy-done = bf16[4,32,512]{2,1,0:T(8,128)(2,1)S(1)} copy-done((bf16[4,32,512]{2,1,0:T(8,128)(2,1)S(1)}, bf16[4,32,512]{2,1,0:T(8,128)(2,1)}, u32[]{:S(2)}) %copy-start) | copy-done | bytes 131096
  0.9 3.0 %collective-permute-start = (bf16[1,2,32,512]{3,2,1,0:T(8,128)(2,1)S(1)}, bf16[1,2,32,512]{3,2,1,0:T(8,128)(2,1)S(1)}, u32[]{:S(2)}, u32[]{:S(2)}) collective-permute-start(bf16[1,2,32,512]{3,2,1,0:T(8,128)(2,1)S(1)} %dynamic-slice_bitcast_fusion), channel_id=1, source_target_pairs={{0,8},{1,9},{2,10},{3,11},{4,12},{5,13},{6,14},{7,15},{8,0},{9,1},... | collective-permute-start | bytes 196616 | tf_op jit(solution)/shard_map/ppermute | solution.py:152
  3.9 2.6 %collective-permute-start.1 = (bf16[1,2,32,512]{3,2,1,0:T(8,128)(2,1)S(1)}, bf16[1,2,32,512]{3,2,1,0:T(8,128)(2,1)S(1)}, u32[]{:S(2)}, u32[]{:S(2)}) collective-permute-start(bf16[1,2,32,512]{3,2,1,0:T(8,128)(2,1)S(1)} %dynamic-slice_bitcast_fusion), channel_id=1, source_target_pairs={{0,16},{1,17},{2,18},{3,19},{4,20},{5,21},{6,22},{7,23},{8,24},{9,... | collective-permute-start | bytes 196616 | tf_op jit(solution)/shard_map/ppermute | solution.py:152
  7.4 1.6 %copy-done.1 = bf16[1,4,512,512]{3,2,1,0:T(8,128)(2,1)S(1)} copy-done((bf16[1,4,512,512]{3,2,1,0:T(8,128)(2,1)S(1)}, bf16[1,4,512,512]{3,2,1,0:T(8,128)(2,1)}, u32[]{:S(2)}) %copy-start.1) | copy-done | bytes 2097176
  9.0 1.2 %copy-done.2 = bf16[1,2,512,512]{3,2,1,0:T(8,128)(2,1)S(1)} copy-done((bf16[1,2,512,512]{3,2,1,0:T(8,128)(2,1)S(1)}, bf16[1,2,512,512]{3,2,1,0:T(8,128)(2,1)}, u32[]{:S(2)}) %copy-start.2) | copy-done | bytes 1048600
  10.2 2.0 %shard_map.73 = (bf16[2,128,512]{2,1,0:T(8,128)(2,1)S(1)}, bf16[2,128,512]{2,1,0:T(8,128)(2,1)S(1)}, bf16[2,256,512]{2,1,0:T(8,128)(2,1)S(1)}, bf16[2,128,128]{2...) custom-call(s32[2]{0:T(128)S(1)} %pad_add_fusion.place, ...), custom_call_target="tpu_custom_call" | custom-call | flops 134217728 | bytes 1048576 | tf_op jit(solution)/shard_map/pallas_call | solution.py:125
  12.6 1.6 %collective-permute-start.3 = (bf16[4,2,32,512]{3,2,1,0:T(8,128)(2,1)S(1)}, bf16[4,2,32,512]{3,2,1,0:T(8,128)(2,1)S(1)}, u32[]{:S(2)}, u32[]{:S(2)}) collective-permute-start(bf16[4,2,32,512]{3,2,1,0:T(8,128)(2,1)S(1)} %pad_maximum_fusion), channel_id=1, source_target_pairs={{0,2},{1,5},{2,0},{3,7},{4,6},{5,1},{6,4},{7,3},{8,10},{9,13},{10,... | collective-permute-start | bytes 786440 | tf_op jit(solution)/shard_map/ppermute | solution.py:152
  14.2 1.5 %collective-permute-start.5 = (bf16[4,2,32,512]{3,2,1,0:T(8,128)(2,1)S(1)}, bf16[4,2,32,512]{3,2,1,0:T(8,128)(2,1)S(1)}, u32[]{:S(2)}, u32[]{:S(2)}) collective-permute-start(bf16[4,2,32,512]{3,2,1,0:T(8,128)(2,1)S(1)} %pad_maximum_fusion), channel_id=1, source_target_pairs={{0,4},{1,3},{2,6},{3,1},{4,0},{5,7},{6,2},{7,5},{8,12},{9,11},{10,... | collective-permute-start | bytes 786440 | tf_op jit(solution)/shard_map/ppermute | solution.py:152
  15.7 5.3 %collective-permute-done.3 = bf16[4,2,32,512]{3,2,1,0:T(8,128)(2,1)S(1)} collective-permute-done((bf16[4,2,32,512]{3,2,1,0:T(8,128)(2,1)S(1)}, bf16[4,2,32,512]{3,2,1,0:T(8,128)(2,1)S(1)}, u32[]{:S(2)}, u32[]{:S(2)}) %collective-permute-start.3) | collective-permute-done | bytes 262176 | tf_op jit(solution)/shard_map/ppermute | solution.py:152
  21.2 1.1 %collective-permute-start.4 = (bf16[4,2,32,512]{3,2,1,0:T(8,128)(2,1)S(1)}, bf16[4,2,32,512]{3,2,1,0:T(8,128)(2,1)S(1)}, u32[]{:S(2)}, u32[]{:S(2)}) collective-permute-start(bf16[4,2,32,512]{3,2,1,0:T(8,128)(2,1)S(1)} %collective-permute-done.3), channel_id=1, source_target_pairs={{0,4},{1,3},{2,6},{3,1},{4,0},{5,7},{6,2},{7,5},{8,12},{9,11},{10,... | collective-permute-start | bytes 786440 | tf_op jit(solution)/shard_map/ppermute | solution.py:152
  22.3 1.2 %collective-permute-done.6.other = bf16[12,2,32,512]{3,2,1,0:T(8,128)(2,1)S(1)} collective-permute-done((bf16[12,2,32,512]{3,2,1,0:T(8,128)(2,1)S(1)}, bf16[12,2,32,512]{3,2,1,0:T(8,128)(2,1)S(1)}, u32[]{:S(2)}, u32[]{:S(2)}) %collective-permute-start.6) | collective-permute-done | bytes 786464 | tf_op jit(solution)/shard_map/ppermute | solution.py:178
  23.5 1.9 %shard_map.74 = (f32[4,128,512]{2,1,0:T(8,128)S(1)}, f32[4,128,512]{2,1,0:T(8,128)S(1)}, f32[4,256,512]{2,1,0:T(8,128)S(1)}) custom-call(s32[4]{0:T(128)S(1)} %get-tuple-element.44.sources, bf16[12,2,32,512]{3,2,1,0:T(8,128)(2,1)S(1)} %constant_dynamic-update-slice_fusion.mine, bf16[12,2,32,512]{3,2,1,0:T(8,128)(2,1)S(1)} %collective-permute-done.6.other, ...), custom_call_target="tpu_custom_call" | custom-call | flops 1073741824 | bytes 1048576 | tf_op jit(solution)/shard_map/pallas_call | solution.py:125
  25.4 2.2 %collective-permute-done.4.mine_last = bf16[4,2,32,512]{3,2,1,0:T(8,128)(2,1)S(1)} collective-permute-done((bf16[4,2,32,512]{3,2,1,0:T(8,128)(2,1)S(1)}, bf16[4,2,32,512]{3,2,1,0:T(8,128)(2,1)S(1)}, u32[]{:S(2)}, u32[]{:S(2)}) %collective-permute-start.4) | collective-permute-done | bytes 262176 | tf_op jit(solution)/shard_map/ppermute | solution.py:152
  29.2 2.0 %shard_map.75 = (bf16[2,128,512]{2,1,0:T(8,128)(2,1)S(1)}, bf16[4,2,32,512]{3,2,1,0:T(8,128)(2,1)S(1)}) custom-call(s32[4]{0:T(128)S(1)} %get-tuple-element.44.sources, s32[1,1,12]{2,1,0:T(1,128)S(1)} %copy-done.3, s32[1,1,12]{2,1,0:T(1,128)S(1)} %copy-done.4, s32[1,1]{1,0:T(1,128)S(6)} %copy.11.live, ...), custom_call_target="tpu_custom_call" | custom-call | flops 805306368 | bytes 1048576 | tf_op jit(solution)/shard_map/pallas_call | solution.py:125
  31.2 1.6 %collective-permute-start.9 = (bf16[4,2,32,512]{3,2,1,0:T(8,128)(2,1)S(1)}, bf16[4,2,32,512]{3,2,1,0:T(8,128)(2,1)S(1)}, u32[]{:S(2)}, u32[]{:S(2)}) collective-permute-start(bf16[4,2,32,512]{3,2,1,0:T(8,128)(2,1)S(1)} %get-tuple-element.62), channel_id=1, source_target_pairs={{0,2},{1,5},{2,0},{3,7},{4,6},{5,1},{6,4},{7,3},{8,10},{9,13},{10,... | collective-permute-start | bytes 786440 | tf_op jit(solution)/shard_map/ppermute | solution.py:152
  32.8 2.0 %shard_map.77 = bf16[4,2,32,512]{3,2,1,0:T(8,128)(2,1)S(1)} custom-call(s32[1,1,12]{2,1,0:T(1,128)S(1)} %copy-done.3, s32[1,1,12]{2,1,0:T(1,128)S(1)} %copy-done.4, s32[1,1]{1,0:T(1,128)S(6)} %copy.11.live, f32[4,128,512]{2,1,0:T(8,128)S(1)} %get-tuple-element.59.early, bf16[2,128,128]{2,1,0:T(8,128)(2,1)S(1)} %get-tuple-element.60.left_last, ...), custom_call_target="tpu_custom_call" | custom-call | flops 805306368 | bytes 1048576 | tf_op jit(solution)/shard_map/pallas_call | solution.py:125
  35.4 3.0 %shard_map.76 = (f32[4,2,32,512]{3,2,1,0:T(8,128)S(1)}, f32[4,2,32,512]{3,2,1,0:T(8,128)S(1)}) custom-call(s32[1,1,12]{2,1,0:T(1,128)S(1)} %copy-done.3, s32[1,1,12]{2,1,0:T(1,128)S(1)} %copy-done.4, s32[1,1]{1,0:T(1,128)S(6)} %copy.11.live, f32[4,256,512]{2,1,0:T(8,128)S(1)} %get-tuple-element.51.early, ...), custom_call_target="tpu_custom_call" | custom-call | flops 1610612736 | bytes 1048576 | tf_op jit(solution)/shard_map/pallas_call | solution.py:125
  38.5 1.1 %collective-permute-start.10 = (bf16[3,2,32,512]{3,2,1,0:T(8,128)(2,1)S(1)}, bf16[3,2,32,512]{3,2,1,0:T(8,128)(2,1)S(1)}, u32[]{:S(2)}, u32[]{:S(2)}) collective-permute-start(bf16[3,2,32,512]{3,2,1,0:T(8,128)(2,1)S(1)} %slice.38), channel_id=1, source_target_pairs={{0,4},{1,3},{2,6},{3,1},{4,0},{5,7},{6,2},{7,5},{8,12},{9,11},{10,... | collective-permute-start | bytes 589832 | tf_op jit(solution)/shard_map/ppermute | solution.py:152
  39.6 2.0 %collective-permute-done.8 = bf16[4,2,32,512]{3,2,1,0:T(8,128)(2,1)S(1)} collective-permute-done((bf16[4,2,32,512]{3,2,1,0:T(8,128)(2,1)S(1)}, bf16[4,2,32,512]{3,2,1,0:T(8,128)(2,1)S(1)}, u32[]{:S(2)}, u32[]{:S(2)}) %collective-permute-start.8) | collective-permute-done | bytes 262176 | tf_op jit(solution)/shard_map/ppermute | solution.py:152
  41.6 2.6 %collective-permute-done.10 = bf16[3,2,32,512]{3,2,1,0:T(8,128)(2,1)S(1)} collective-permute-done((bf16[3,2,32,512]{3,2,1,0:T(8,128)(2,1)S(1)}, bf16[3,2,32,512]{3,2,1,0:T(8,128)(2,1)S(1)}, u32[]{:S(2)}, u32[]{:S(2)}) %collective-permute-start.10) | collective-permute-done | bytes 196640 | tf_op jit(solution)/shard_map/ppermute | solution.py:152
  44.3 1.7 %collective-permute-start.12 = (bf16[2,32,512]{2,1,0:T(8,128)(2,1)S(1)}, bf16[2,32,512]{2,1,0:T(8,128)(2,1)S(1)}, u32[]{:S(2)}, u32[]{:S(2)}) collective-permute-start(bf16[2,32,512]{2,1,0:T(8,128)(2,1)S(1)} %get-tuple-element.65), channel_id=1, source_target_pairs={{0,16},{1,17},{2,18},{3,19},{4,20},{5,21},{6,22},{7,23},{8,24},{9,... | collective-permute-start | bytes 196616 | tf_op jit(solution)/shard_map/ppermute | solution.py:152
  46.0 2.0 %collective-permute-start.13 = (bf16[2,32,512]{2,1,0:T(8,128)(2,1)S(1)}, bf16[2,32,512]{2,1,0:T(8,128)(2,1)S(1)}, u32[]{:S(2)}, u32[]{:S(2)}) collective-permute-start(bf16[2,32,512]{2,1,0:T(8,128)(2,1)S(1)} %get-tuple-element.67), channel_id=1, source_target_pairs={{0,24},{1,25},{2,26},{3,27},{4,28},{5,29},{6,30},{7,31},{8,16},{9,... | collective-permute-start | bytes 196616 | tf_op jit(solution)/shard_map/ppermute | solution.py:152
  49.4 1.7 %collective-permute-done.12 = bf16[2,32,512]{2,1,0:T(8,128)(2,1)S(1)} collective-permute-done((bf16[2,32,512]{2,1,0:T(8,128)(2,1)S(1)}, bf16[2,32,512]{2,1,0:T(8,128)(2,1)S(1)}, u32[]{:S(2)}, u32[]{:S(2)}) %collective-permute-start.12) | collective-permute-done | bytes 65568 | tf_op jit(solution)/shard_map/ppermute | solution.py:152
  51.1 1.1 %collective-permute-done.13 = bf16[2,32,512]{2,1,0:T(8,128)(2,1)S(1)} collective-permute-done((bf16[2,32,512]{2,1,0:T(8,128)(2,1)S(1)}, bf16[2,32,512]{2,1,0:T(8,128)(2,1)S(1)}, u32[]{:S(2)}, u32[]{:S(2)}) %collective-permute-start.13) | collective-permute-done | bytes 65568 | tf_op jit(solution)/shard_map/ppermute | solution.py:152
  (34 shorter events, 5.8 us)
Async XLA Ops:
  0.0 0.9 %copy-start = (bf16[4,32,512]{2,1,0:T(8,128)(2,1)S(1)}, bf16[4,32,512]{2,1,0:T(8,128)(2,1)}, u32[]{:S(2)}) copy-start(bf16[4,32,512]{2,1,0:T(8,128)(2,1)} %param.7) | copy-start | bytes 393220
  0.9 11.3 %collective-permute-start = (bf16[1,2,32,512]{3,2,1,0:T(8,128)(2,1)S(1)}, bf16[1,2,32,512]{3,2,1,0:T(8,128)(2,1)S(1)}, u32[]{:S(2)}, u32[]{:S(2)}) collective-permute-start(bf16[1,2,32,512]{3,2,1,0:T(8,128)(2,1)S(1)} %dynamic-slice_bitcast_fusion), channel_id=1, source_target_pairs={{0,8},{1,9},{2,10},{3,11},{4,12},{5,13},{6,14},{7,15},{8,0},{9,1},... | collective-permute-start | bytes 196616 | tf_op jit(solution)/shard_map/ppermute | solution.py:152
  3.9 8.2 %collective-permute-start.1 = (bf16[1,2,32,512]{3,2,1,0:T(8,128)(2,1)S(1)}, bf16[1,2,32,512]{3,2,1,0:T(8,128)(2,1)S(1)}, u32[]{:S(2)}, u32[]{:S(2)}) collective-permute-start(bf16[1,2,32,512]{3,2,1,0:T(8,128)(2,1)S(1)} %dynamic-slice_bitcast_fusion), channel_id=1, source_target_pairs={{0,16},{1,17},{2,18},{3,19},{4,20},{5,21},{6,22},{7,23},{8,24},{9,... | collective-permute-start | bytes 196616 | tf_op jit(solution)/shard_map/ppermute | solution.py:152
  6.5 6.1 %collective-permute-start.2 = (bf16[1,2,32,512]{3,2,1,0:T(8,128)(2,1)S(1)}, bf16[1,2,32,512]{3,2,1,0:T(8,128)(2,1)S(1)}, u32[]{:S(2)}, u32[]{:S(2)}) collective-permute-start(bf16[1,2,32,512]{3,2,1,0:T(8,128)(2,1)S(1)} %dynamic-slice_bitcast_fusion), channel_id=1, source_target_pairs={{0,24},{1,25},{2,26},{3,27},{4,28},{5,29},{6,30},{7,31},{8,16},{9,... | collective-permute-start | bytes 196616 | tf_op jit(solution)/shard_map/ppermute | solution.py:152
  7.4 1.6 %copy-start.1 = (bf16[1,4,512,512]{3,2,1,0:T(8,128)(2,1)S(1)}, bf16[1,4,512,512]{3,2,1,0:T(8,128)(2,1)}, u32[]{:S(2)}) copy-start(bf16[1,4,512,512]{3,2,1,0:T(8,128)(2,1)} %right.1) | copy-start | bytes 6291460
  9.0 1.2 %copy-start.2 = (bf16[1,2,512,512]{3,2,1,0:T(8,128)(2,1)S(1)}, bf16[1,2,512,512]{3,2,1,0:T(8,128)(2,1)}, u32[]{:S(2)}) copy-start(bf16[1,2,512,512]{3,2,1,0:T(8,128)(2,1)} %left.1) | copy-start | bytes 3145732
  12.6 8.4 %collective-permute-start.3 = (bf16[4,2,32,512]{3,2,1,0:T(8,128)(2,1)S(1)}, bf16[4,2,32,512]{3,2,1,0:T(8,128)(2,1)S(1)}, u32[]{:S(2)}, u32[]{:S(2)}) collective-permute-start(bf16[4,2,32,512]{3,2,1,0:T(8,128)(2,1)S(1)} %pad_maximum_fusion), channel_id=1, source_target_pairs={{0,2},{1,5},{2,0},{3,7},{4,6},{5,1},{6,4},{7,3},{8,10},{9,13},{10,... | collective-permute-start | bytes 786440 | tf_op jit(solution)/shard_map/ppermute | solution.py:152
  14.2 6.9 %collective-permute-start.5 = (bf16[4,2,32,512]{3,2,1,0:T(8,128)(2,1)S(1)}, bf16[4,2,32,512]{3,2,1,0:T(8,128)(2,1)S(1)}, u32[]{:S(2)}, u32[]{:S(2)}) collective-permute-start(bf16[4,2,32,512]{3,2,1,0:T(8,128)(2,1)S(1)} %pad_maximum_fusion), channel_id=1, source_target_pairs={{0,4},{1,3},{2,6},{3,1},{4,0},{5,7},{6,2},{7,5},{8,12},{9,11},{10,... | collective-permute-start | bytes 786440 | tf_op jit(solution)/shard_map/ppermute | solution.py:152
  21.1 8.1 %copy-start.3 = (s32[1,1,12]{2,1,0:T(1,128)S(1)}, s32[1,1,12]{2,1,0:T(1,128)}, u32[]{:S(2)}) copy-start(s32[1,1,12]{2,1,0:T(1,128)} %pairs.5) | copy-start | bytes 148
  21.1 8.1 %copy-start.4 = (s32[1,1,12]{2,1,0:T(1,128)S(1)}, s32[1,1,12]{2,1,0:T(1,128)}, u32[]{:S(2)}) copy-start(s32[1,1,12]{2,1,0:T(1,128)} %targets.5) | copy-start | bytes 148
  21.1 2.4 %collective-permute-start.6 = (bf16[12,2,32,512]{3,2,1,0:T(8,128)(2,1)S(1)}, bf16[12,2,32,512]{3,2,1,0:T(8,128)(2,1)S(1)}, u32[]{:S(2)}, u32[]{:S(2)}) collective-permute-start(bf16[12,2,32,512]{3,2,1,0:T(8,128)(2,1)S(1)} %constant_dynamic-update-slice_fusion.mine), channel_id=1, source_target_pairs={{0,1},{1,0},{2,3},{3,2},{4,5},{5,4},{6,7},{7,6},{8,9},{9,8},{10,11... | collective-permute-start | bytes 2359304 | tf_op jit(solution)/shard_map/ppermute | solution.py:178
  21.2 6.4 %collective-permute-start.4 = (bf16[4,2,32,512]{3,2,1,0:T(8,128)(2,1)S(1)}, bf16[4,2,32,512]{3,2,1,0:T(8,128)(2,1)S(1)}, u32[]{:S(2)}, u32[]{:S(2)}) collective-permute-start(bf16[4,2,32,512]{3,2,1,0:T(8,128)(2,1)S(1)} %collective-permute-done.3), channel_id=1, source_target_pairs={{0,4},{1,3},{2,6},{3,1},{4,0},{5,7},{6,2},{7,5},{8,12},{9,11},{10,... | collective-permute-start | bytes 786440 | tf_op jit(solution)/shard_map/ppermute | solution.py:152
  27.6 1.5 %collective-permute-start.7 = (bf16[4,2,32,512]{3,2,1,0:T(8,128)(2,1)S(1)}, bf16[4,2,32,512]{3,2,1,0:T(8,128)(2,1)S(1)}, u32[]{:S(2)}, u32[]{:S(2)}) collective-permute-start(bf16[4,2,32,512]{3,2,1,0:T(8,128)(2,1)S(1)} %collective-permute-done.4.mine_last), channel_id=1, source_target_pairs={{0,1},{1,0},{2,3},{3,2},{4,5},{5,4},{6,7},{7,6},{8,9},{9,8},{10,11... | collective-permute-start | bytes 786440 | tf_op jit(solution)/shard_map/ppermute | solution.py:186
  31.2 7.1 %collective-permute-start.9 = (bf16[4,2,32,512]{3,2,1,0:T(8,128)(2,1)S(1)}, bf16[4,2,32,512]{3,2,1,0:T(8,128)(2,1)S(1)}, u32[]{:S(2)}, u32[]{:S(2)}) collective-permute-start(bf16[4,2,32,512]{3,2,1,0:T(8,128)(2,1)S(1)} %get-tuple-element.62), channel_id=1, source_target_pairs={{0,2},{1,5},{2,0},{3,7},{4,6},{5,1},{6,4},{7,3},{8,10},{9,13},{10,... | collective-permute-start | bytes 786440 | tf_op jit(solution)/shard_map/ppermute | solution.py:152
  34.8 6.9 %collective-permute-start.8 = (bf16[4,2,32,512]{3,2,1,0:T(8,128)(2,1)S(1)}, bf16[4,2,32,512]{3,2,1,0:T(8,128)(2,1)S(1)}, u32[]{:S(2)}, u32[]{:S(2)}) collective-permute-start(bf16[4,2,32,512]{3,2,1,0:T(8,128)(2,1)S(1)} %shard_map.77), channel_id=1, source_target_pairs={{0,2},{1,5},{2,0},{3,7},{4,6},{5,1},{6,4},{7,3},{8,10},{9,13},{10,... | collective-permute-start | bytes 786440 | tf_op jit(solution)/shard_map/ppermute | solution.py:152
  38.5 5.7 %collective-permute-start.10 = (bf16[3,2,32,512]{3,2,1,0:T(8,128)(2,1)S(1)}, bf16[3,2,32,512]{3,2,1,0:T(8,128)(2,1)S(1)}, u32[]{:S(2)}, u32[]{:S(2)}) collective-permute-start(bf16[3,2,32,512]{3,2,1,0:T(8,128)(2,1)S(1)} %slice.38), channel_id=1, source_target_pairs={{0,4},{1,3},{2,6},{3,1},{4,0},{5,7},{6,2},{7,5},{8,12},{9,11},{10,... | collective-permute-start | bytes 589832 | tf_op jit(solution)/shard_map/ppermute | solution.py:152
  44.3 6.8 %collective-permute-start.12 = (bf16[2,32,512]{2,1,0:T(8,128)(2,1)S(1)}, bf16[2,32,512]{2,1,0:T(8,128)(2,1)S(1)}, u32[]{:S(2)}, u32[]{:S(2)}) collective-permute-start(bf16[2,32,512]{2,1,0:T(8,128)(2,1)S(1)} %get-tuple-element.65), channel_id=1, source_target_pairs={{0,16},{1,17},{2,18},{3,19},{4,20},{5,21},{6,22},{7,23},{8,24},{9,... | collective-permute-start | bytes 196616 | tf_op jit(solution)/shard_map/ppermute | solution.py:152
  46.0 6.2 %collective-permute-start.13 = (bf16[2,32,512]{2,1,0:T(8,128)(2,1)S(1)}, bf16[2,32,512]{2,1,0:T(8,128)(2,1)S(1)}, u32[]{:S(2)}, u32[]{:S(2)}) collective-permute-start(bf16[2,32,512]{2,1,0:T(8,128)(2,1)S(1)} %get-tuple-element.67), channel_id=1, source_target_pairs={{0,24},{1,25},{2,26},{3,27},{4,28},{5,29},{6,30},{7,31},{8,16},{9,... | collective-permute-start | bytes 196616 | tf_op jit(solution)/shard_map/ppermute | solution.py:152
  48.0 4.9 %collective-permute-start.14 = (bf16[2,32,512]{2,1,0:T(8,128)(2,1)S(1)}, bf16[2,32,512]{2,1,0:T(8,128)(2,1)S(1)}, u32[]{:S(2)}, u32[]{:S(2)}) collective-permute-start(bf16[2,32,512]{2,1,0:T(8,128)(2,1)S(1)} %get-tuple-element.66), channel_id=1, source_target_pairs={{0,8},{1,9},{2,10},{3,11},{4,12},{5,13},{6,14},{7,15},{8,0},{9,1},... | collective-permute-start | bytes 196616 | tf_op jit(solution)/shard_map/ppermute | solution.py:152
  48.5 4.4 %collective-permute-start.11 = (bf16[2,32,512]{2,1,0:T(8,128)(2,1)S(1)}, bf16[2,32,512]{2,1,0:T(8,128)(2,1)S(1)}, u32[]{:S(2)}, u32[]{:S(2)}) collective-permute-start(bf16[2,32,512]{2,1,0:T(8,128)(2,1)S(1)} %slice_bitcast_fusion), channel_id=1, source_target_pairs={{0,4},{1,3},{2,6},{3,1},{4,0},{5,7},{6,2},{7,5},{8,12},{9,11},{10,... | collective-permute-start | bytes 196616 | tf_op jit(solution)/shard_map/ppermute | solution.py:152

commit v4 on v3

--- a/solution.py
+++ b/solution.py
@@ -1,4 +1,5 @@
 import functools
+import math
 
 import jax
 import jax.numpy as jnp
@@ -12,7 +13,7 @@
 F32 = jnp.float32
 VMEM = pl.BlockSpec(memory_space=pltpu.VMEM)
 SMEM = pl.BlockSpec(memory_space=pltpu.SMEM)
-VMEM_BYTES = 24 * 2**20
+SPARE_BYTES = 4 * 2**20
 GROUPS = ((3,), (1,), (2, 0))
 
 
@@ -122,13 +123,15 @@
     def spec(array):
         return SMEM if jnp.issubdtype(array.dtype, jnp.integer) else VMEM
 
+    held = [*operands, *out_shapes, *scratch_shapes]
+    need_bytes = sum(math.prod(array.shape) * jnp.dtype(array.dtype).itemsize for array in held)
     return pl.pallas_call(
         kernel,
         out_shape=out_shapes,
         in_specs=[spec(operand) for operand in operands],
         out_specs=[spec(out) for out in out_shapes],
         scratch_shapes=scratch_shapes,
-        compiler_params=pltpu.CompilerParams(vmem_limit_bytes=VMEM_BYTES),
+        compiler_params=pltpu.CompilerParams(vmem_limit_bytes=need_bytes + SPARE_BYTES),
         cost_estimate=pl.CostEstimate(flops=flops, bytes_accessed=2**20, transcendentals=0),
     )(*operands)
 
@@ -156,7 +159,11 @@
 
     work_type = BF16 if rows % 16 == 0 else F32
     used = [len(group) * quarter for group in GROUPS]
+    own = lax.dynamic_slice_in_dim(wave_blocks, core * half, half, 0)[None]
+    by_level = {k: swap(own, none, k) for k in far_first}
+    line = jnp.concatenate([own] + [by_level[k] for k in range(1, depth)], 0)
     place = jnp.stack([me, core]).astype(jnp.int32)
+    place, line = lax.optimization_barrier((place, line))
     *prepared, sources = call(
         functools.partial(prepare_kernel, rows),
         [shape((ops_l, u, size), work_type) for u in used]
@@ -165,14 +172,10 @@
         [pltpu.VMEM((size, max(used)), work_type), pltpu.VMEM((quarter, max(used)), work_type)],
         size**3, place, wanted, left_ops.astype(work_type), right_ops,
     )
-
-    own = lax.dynamic_slice_in_dim(wave_blocks, core * half, half, 0)[None]
-    by_level = {k: swap(own, none, k) for k in far_first}
-    line = jnp.concatenate([own] + [by_level[k] for k in range(1, depth)], 0)
-    line, prepared, sources = lax.optimization_barrier((line, prepared, sources))
-    lefts, lasts, turned = prepared[:len(GROUPS)], prepared[len(GROUPS):-1], prepared[-1]
     from_first = swap(line, first)
     from_second = swap(line, second)
+    from_first, from_second, prepared, sources = lax.optimization_barrier((from_first, from_second, prepared, sources))
+    lefts, lasts, turned = prepared[:len(GROUPS)], prepared[len(GROUPS):-1], prepared[-1]
     mine_last = swap(from_first, second)
     mine = jnp.concatenate([line, from_first, from_second], 0)
     other = lax.ppermute(mine, AXES, across)

time: 53.8 us -> 52.9 us (0.983)
  starting transfers between devices: 18.2 us -> 16.9 us
  waiting for transfers between devices: 18.1 us -> 19 us
    ppermute x13, starting transfers between devices: 18.1 us -> 16.8 us  [swap(): return lax.ppermute(array, AXES, pairs_of)]
    ppermute x13, waiting for transfers between devices: 16.1 us -> 16.7 us  [swap(): return lax.ppermute(array, AXES, pairs_of)]
  transfers between devices with their start and end apart: 15 -> 15, of which waited for: 10 -> 10; matrix products, arithmetic and copies ran while one was open for 2% -> 2% of each run, Pallas kernels for 17% -> 16%
where the time goes in v4:
time: 52.9 us; the launch traced here: 52.7 us
  waiting for transfers between devices  19 us (36%)
  starting transfers between devices  16.9 us (32%)
  Pallas kernels  10.4 us (20%)
  local copies, waits for them, and re-layouts  4.58 us (9%)
  other arithmetic  0.99 us (2%)
  between operations  0.81 us (2%)
    ppermute x13, starting transfers between devices, swap(): return lax.ppermute(array, AXES, pairs_of)  16.8 us
    ppermute x13, waiting for transfers between devices, swap(): return lax.ppermute(array, AXES, pairs_of)  16.7 us
    pallas_call x5, Pallas kernels, call(): pl.pallas_call(kernel, out_shape=out_shapes, in_specs=[spec(operand) for...  10.4 us
    unnamed x13, local copies, waits for them, and re-layouts  4.52 us
    ppermute x1, waiting for transfers between devices, on_device(): other = lax.ppermute(mine, AXES, across)  1.44 us
  transfers between devices with their start and end apart: 15, of which 10 were waited for; matrix products, arithmetic and copies ran while one was open for 2% of the time, Pallas kernels for 16%

profile of v4, /device:TPU:0, one launch (start us, length us, event | category | flops | bytes accessed | tf_op | source)
XLA Modules:
  0.0 52.7 jit_solution(7201227509445257768)
XLA Ops:
  0.0 0.9 %copy-done = bf16[4,32,512]{2,1,0:T(8,128)(2,1)S(1)} copy-done((bf16[4,32,512]{2,1,0:T(8,128)(2,1)S(1)}, bf16[4,32,512]{2,1,0:T(8,128)(2,1)}, u32[]{:S(2)}) %copy-start) | copy-done | bytes 131096
  0.9 3.0 %collective-permute-start = (bf16[1,2,32,512]{3,2,1,0:T(8,128)(2,1)S(1)}, bf16[1,2,32,512]{3,2,1,0:T(8,128)(2,1)S(1)}, u32[]{:S(2)}, u32[]{:S(2)}) collective-permute-start(bf16[1,2,32,512]{3,2,1,0:T(8,128)(2,1)S(1)} %dynamic-slice_bitcast_fusion), channel_id=1, source_target_pairs={{0,8},{1,9},{2,10},{3,11},{4,12},{5,13},{6,14},{7,15},{8,0},{9,1},... | collective-permute-start | bytes 196616 | tf_op jit(solution)/shard_map/ppermute | solution.py:155
  3.9 2.6 %collective-permute-start.1 = (bf16[1,2,32,512]{3,2,1,0:T(8,128)(2,1)S(1)}, bf16[1,2,32,512]{3,2,1,0:T(8,128)(2,1)S(1)}, u32[]{:S(2)}, u32[]{:S(2)}) collective-permute-start(bf16[1,2,32,512]{3,2,1,0:T(8,128)(2,1)S(1)} %dynamic-slice_bitcast_fusion), channel_id=1, source_target_pairs={{0,16},{1,17},{2,18},{3,19},{4,20},{5,21},{6,22},{7,23},{8,24},{9,... | collective-permute-start | bytes 196616 | tf_op jit(solution)/shard_map/ppermute | solution.py:155
  6.6 4.6 %collective-permute-done.1 = bf16[1,2,32,512]{3,2,1,0:T(8,128)(2,1)S(1)} collective-permute-done((bf16[1,2,32,512]{3,2,1,0:T(8,128)(2,1)S(1)}, bf16[1,2,32,512]{3,2,1,0:T(8,128)(2,1)S(1)}, u32[]{:S(2)}, u32[]{:S(2)}) %collective-permute-start.1) | collective-permute-done | bytes 65568 | tf_op jit(solution)/shard_map/ppermute | solution.py:155
  11.2 1.4 %collective-permute-done.2 = bf16[1,2,32,512]{3,2,1,0:T(8,128)(2,1)S(1)} collective-permute-done((bf16[1,2,32,512]{3,2,1,0:T(8,128)(2,1)S(1)}, bf16[1,2,32,512]{3,2,1,0:T(8,128)(2,1)S(1)}, u32[]{:S(2)}, u32[]{:S(2)}) %collective-permute-start.2) | collective-permute-done | bytes 65568 | tf_op jit(solution)/shard_map/ppermute | solution.py:155
  12.6 1.6 %collective-permute-start.3 = (bf16[4,2,32,512]{3,2,1,0:T(8,128)(2,1)S(1)}, bf16[4,2,32,512]{3,2,1,0:T(8,128)(2,1)S(1)}, u32[]{:S(2)}, u32[]{:S(2)}) collective-permute-start(bf16[4,2,32,512]{3,2,1,0:T(8,128)(2,1)S(1)} %pad_maximum_fusion), channel_id=1, source_target_pairs={{0,2},{1,5},{2,0},{3,7},{4,6},{5,1},{6,4},{7,3},{8,10},{9,13},{10,... | collective-permute-start | bytes 786440 | tf_op jit(solution)/shard_map/ppermute | solution.py:155
  14.2 1.5 %collective-permute-start.4 = (bf16[4,2,32,512]{3,2,1,0:T(8,128)(2,1)S(1)}, bf16[4,2,32,512]{3,2,1,0:T(8,128)(2,1)S(1)}, u32[]{:S(2)}, u32[]{:S(2)}) collective-permute-start(bf16[4,2,32,512]{3,2,1,0:T(8,128)(2,1)S(1)} %pad_maximum_fusion), channel_id=1, source_target_pairs={{0,4},{1,3},{2,6},{3,1},{4,0},{5,7},{6,2},{7,5},{8,12},{9,11},{10,... | collective-permute-start | bytes 786440 | tf_op jit(solution)/shard_map/ppermute | solution.py:155
  16.5 1.6 %copy-done.1 = bf16[1,4,512,512]{3,2,1,0:T(8,128)(2,1)S(1)} copy-done((bf16[1,4,512,512]{3,2,1,0:T(8,128)(2,1)S(1)}, bf16[1,4,512,512]{3,2,1,0:T(8,128)(2,1)}, u32[]{:S(2)}) %copy-start.1) | copy-done | bytes 2097176
  18.1 1.2 %copy-done.2 = bf16[1,2,512,512]{3,2,1,0:T(8,128)(2,1)S(1)} copy-done((bf16[1,2,512,512]{3,2,1,0:T(8,128)(2,1)S(1)}, bf16[1,2,512,512]{3,2,1,0:T(8,128)(2,1)}, u32[]{:S(2)}) %copy-start.2) | copy-done | bytes 1048600
  19.3 2.0 %shard_map.73 = (bf16[2,128,512]{2,1,0:T(8,128)(2,1)S(1)}, bf16[2,128,512]{2,1,0:T(8,128)(2,1)S(1)}, bf16[2,256,512]{2,1,0:T(8,128)(2,1)S(1)}, bf16[2,128,128]{2...) custom-call(s32[2]{0:T(128)S(1)} %pad_add_fusion.place, ...), custom_call_target="tpu_custom_call" | custom-call | flops 134217728 | bytes 1048576 | tf_op jit(solution)/shard_map/pallas_call | solution.py:128
  22.3 1.4 %collective-permute-done.6.other = bf16[12,2,32,512]{3,2,1,0:T(8,128)(2,1)S(1)} collective-permute-done((bf16[12,2,32,512]{3,2,1,0:T(8,128)(2,1)S(1)}, bf16[12,2,32,512]{3,2,1,0:T(8,128)(2,1)S(1)}, u32[]{:S(2)}, u32[]{:S(2)}) %collective-permute-start.6) | collective-permute-done | bytes 786464 | tf_op jit(solution)/shard_map/ppermute | solution.py:181
  23.8 1.9 %shard_map.74 = (f32[4,128,512]{2,1,0:T(8,128)S(1)}, f32[4,128,512]{2,1,0:T(8,128)S(1)}, f32[4,256,512]{2,1,0:T(8,128)S(1)}) custom-call(s32[4]{0:T(128)S(1)} %get-tuple-element.49.sources, bf16[12,2,32,512]{3,2,1,0:T(8,128)(2,1)S(1)} %constant_dynamic-update-slice_fusion.mine, bf16[12,2,32,512]{3,2,1,0:T(8,128)(2,1)S(1)} %collective-permute-done.6.other, ...), custom_call_target="tpu_custom_call" | custom-call | flops 1073741824 | bytes 1048576 | tf_op jit(solution)/shard_map/pallas_call | solution.py:128
  25.7 2.2 %collective-permute-done.5.mine_last = bf16[4,2,32,512]{3,2,1,0:T(8,128)(2,1)S(1)} collective-permute-done((bf16[4,2,32,512]{3,2,1,0:T(8,128)(2,1)S(1)}, bf16[4,2,32,512]{3,2,1,0:T(8,128)(2,1)S(1)}, u32[]{:S(2)}, u32[]{:S(2)}) %collective-permute-start.5) | collective-permute-done | bytes 262176 | tf_op jit(solution)/shard_map/ppermute | solution.py:155
  28.6 0.9 %collective-permute-done.7.other_last = bf16[4,2,32,512]{3,2,1,0:T(8,128)(2,1)S(1)} collective-permute-done((bf16[4,2,32,512]{3,2,1,0:T(8,128)(2,1)S(1)}, bf16[4,2,32,512]{3,2,1,0:T(8,128)(2,1)S(1)}, u32[]{:S(2)}, u32[]{:S(2)}) %collective-permute-start.7) | collective-permute-done | bytes 262176 | tf_op jit(solution)/shard_map/ppermute | solution.py:189
  29.5 1.9 %shard_map.75 = (bf16[2,128,512]{2,1,0:T(8,128)(2,1)S(1)}, bf16[4,2,32,512]{3,2,1,0:T(8,128)(2,1)S(1)}) custom-call(s32[4]{0:T(128)S(1)} %get-tuple-element.49.sources, s32[1,1,12]{2,1,0:T(1,128)S(1)} %copy-done.3, s32[1,1,12]{2,1,0:T(1,128)S(1)} %copy-done.4, s32[1,1]{1,0:T(1,128)S(6)} %copy.11.live, ...), custom_call_target="tpu_custom_call" | custom-call | flops 805306368 | bytes 1048576 | tf_op jit(solution)/shard_map/pallas_call | solution.py:128
  32.0 1.8 %shard_map.77 = bf16[4,2,32,512]{3,2,1,0:T(8,128)(2,1)S(1)} custom-call(s32[1,1,12]{2,1,0:T(1,128)S(1)} %copy-done.3, s32[1,1,12]{2,1,0:T(1,128)S(1)} %copy-done.4, s32[1,1]{1,0:T(1,128)S(6)} %copy.11.live, f32[4,128,512]{2,1,0:T(8,128)S(1)} %get-tuple-element.65.early, bf16[2,128,128]{2,1,0:T(8,128)(2,1)S(1)} %get-tuple-element.66.left_last, ...), custom_call_target="tpu_custom_call" | custom-call | flops 805306368 | bytes 1048576 | tf_op jit(solution)/shard_map/pallas_call | solution.py:128
  33.8 1.6 %collective-permute-start.8 = (bf16[4,2,32,512]{3,2,1,0:T(8,128)(2,1)S(1)}, bf16[4,2,32,512]{3,2,1,0:T(8,128)(2,1)S(1)}, u32[]{:S(2)}, u32[]{:S(2)}) collective-permute-start(bf16[4,2,32,512]{3,2,1,0:T(8,128)(2,1)S(1)} %shard_map.77), channel_id=1, source_target_pairs={{0,2},{1,5},{2,0},{3,7},{4,6},{5,1},{6,4},{7,3},{8,10},{9,13},{10,... | collective-permute-start | bytes 786440 | tf_op jit(solution)/shard_map/ppermute | solution.py:155
  35.4 2.8 %shard_map.76 = (f32[4,2,32,512]{3,2,1,0:T(8,128)S(1)}, f32[4,2,32,512]{3,2,1,0:T(8,128)S(1)}) custom-call(s32[1,1,12]{2,1,0:T(1,128)S(1)} %copy-done.3, s32[1,1,12]{2,1,0:T(1,128)S(1)} %copy-done.4, s32[1,1]{1,0:T(1,128)S(6)} %copy.11.live, f32[4,256,512]{2,1,0:T(8,128)S(1)} %get-tuple-element.57.early, ...), custom_call_target="tpu_custom_call" | custom-call | flops 1610612736 | bytes 1048576 | tf_op jit(solution)/shard_map/pallas_call | solution.py:128
  39.1 1.5 %collective-permute-done.8 = bf16[4,2,32,512]{3,2,1,0:T(8,128)(2,1)S(1)} collective-permute-done((bf16[4,2,32,512]{3,2,1,0:T(8,128)(2,1)S(1)}, bf16[4,2,32,512]{3,2,1,0:T(8,128)(2,1)S(1)}, u32[]{:S(2)}, u32[]{:S(2)}) %collective-permute-start.8) | collective-permute-done | bytes 262176 | tf_op jit(solution)/shard_map/ppermute | solution.py:155
  40.6 3.4 %collective-permute-done.10 = bf16[3,2,32,512]{3,2,1,0:T(8,128)(2,1)S(1)} collective-permute-done((bf16[3,2,32,512]{3,2,1,0:T(8,128)(2,1)S(1)}, bf16[3,2,32,512]{3,2,1,0:T(8,128)(2,1)S(1)}, u32[]{:S(2)}, u32[]{:S(2)}) %collective-permute-start.10) | collective-permute-done | bytes 196640 | tf_op jit(solution)/shard_map/ppermute | solution.py:155
  44.2 1.6 %collective-permute-start.12 = (bf16[2,32,512]{2,1,0:T(8,128)(2,1)S(1)}, bf16[2,32,512]{2,1,0:T(8,128)(2,1)S(1)}, u32[]{:S(2)}, u32[]{:S(2)}) collective-permute-start(bf16[2,32,512]{2,1,0:T(8,128)(2,1)S(1)} %get-tuple-element.71), channel_id=1, source_target_pairs={{0,16},{1,17},{2,18},{3,19},{4,20},{5,21},{6,22},{7,23},{8,24},{9,... | collective-permute-start | bytes 196616 | tf_op jit(solution)/shard_map/ppermute | solution.py:155
  46.5 1.3 %collective-permute-start.14 = (bf16[2,32,512]{2,1,0:T(8,128)(2,1)S(1)}, bf16[2,32,512]{2,1,0:T(8,128)(2,1)S(1)}, u32[]{:S(2)}, u32[]{:S(2)}) collective-permute-start(bf16[2,32,512]{2,1,0:T(8,128)(2,1)S(1)} %get-tuple-element.72), channel_id=1, source_target_pairs={{0,8},{1,9},{2,10},{3,11},{4,12},{5,13},{6,14},{7,15},{8,0},{9,1},... | collective-permute-start | bytes 196616 | tf_op jit(solution)/shard_map/ppermute | solution.py:155
  48.5 2.0 %collective-permute-done.12 = bf16[2,32,512]{2,1,0:T(8,128)(2,1)S(1)} collective-permute-done((bf16[2,32,512]{2,1,0:T(8,128)(2,1)S(1)}, bf16[2,32,512]{2,1,0:T(8,128)(2,1)S(1)}, u32[]{:S(2)}, u32[]{:S(2)}) %collective-permute-start.12) | collective-permute-done | bytes 65568 | tf_op jit(solution)/shard_map/ppermute | solution.py:155
  50.5 1.4 %collective-permute-done.13 = bf16[2,32,512]{2,1,0:T(8,128)(2,1)S(1)} collective-permute-done((bf16[2,32,512]{2,1,0:T(8,128)(2,1)S(1)}, bf16[2,32,512]{2,1,0:T(8,128)(2,1)S(1)}, u32[]{:S(2)}, u32[]{:S(2)}) %collective-permute-start.13) | collective-permute-done | bytes 65568 | tf_op jit(solution)/shard_map/ppermute | solution.py:155
  (34 shorter events, 5.7 us)
Async XLA Ops:
  0.0 0.9 %copy-start = (bf16[4,32,512]{2,1,0:T(8,128)(2,1)S(1)}, bf16[4,32,512]{2,1,0:T(8,128)(2,1)}, u32[]{:S(2)}) copy-start(bf16[4,32,512]{2,1,0:T(8,128)(2,1)} %param.7) | copy-start | bytes 393220
  0.9 5.7 %collective-permute-start = (bf16[1,2,32,512]{3,2,1,0:T(8,128)(2,1)S(1)}, bf16[1,2,32,512]{3,2,1,0:T(8,128)(2,1)S(1)}, u32[]{:S(2)}, u32[]{:S(2)}) collective-permute-start(bf16[1,2,32,512]{3,2,1,0:T(8,128)(2,1)S(1)} %dynamic-slice_bitcast_fusion), channel_id=1, source_target_pairs={{0,8},{1,9},{2,10},{3,11},{4,12},{5,13},{6,14},{7,15},{8,0},{9,1},... | collective-permute-start | bytes 196616 | tf_op jit(solution)/shard_map/ppermute | solution.py:155
  3.9 7.3 %collective-permute-start.1 = (bf16[1,2,32,512]{3,2,1,0:T(8,128)(2,1)S(1)}, bf16[1,2,32,512]{3,2,1,0:T(8,128)(2,1)S(1)}, u32[]{:S(2)}, u32[]{:S(2)}) collective-permute-start(bf16[1,2,32,512]{3,2,1,0:T(8,128)(2,1)S(1)} %dynamic-slice_bitcast_fusion), channel_id=1, source_target_pairs={{0,16},{1,17},{2,18},{3,19},{4,20},{5,21},{6,22},{7,23},{8,24},{9,... | collective-permute-start | bytes 196616 | tf_op jit(solution)/shard_map/ppermute | solution.py:155
  6.5 6.1 %collective-permute-start.2 = (bf16[1,2,32,512]{3,2,1,0:T(8,128)(2,1)S(1)}, bf16[1,2,32,512]{3,2,1,0:T(8,128)(2,1)S(1)}, u32[]{:S(2)}, u32[]{:S(2)}) collective-permute-start(bf16[1,2,32,512]{3,2,1,0:T(8,128)(2,1)S(1)} %dynamic-slice_bitcast_fusion), channel_id=1, source_target_pairs={{0,24},{1,25},{2,26},{3,27},{4,28},{5,29},{6,30},{7,31},{8,16},{9,... | collective-permute-start | bytes 196616 | tf_op jit(solution)/shard_map/ppermute | solution.py:155
  12.6 8.7 %collective-permute-start.3 = (bf16[4,2,32,512]{3,2,1,0:T(8,128)(2,1)S(1)}, bf16[4,2,32,512]{3,2,1,0:T(8,128)(2,1)S(1)}, u32[]{:S(2)}, u32[]{:S(2)}) collective-permute-start(bf16[4,2,32,512]{3,2,1,0:T(8,128)(2,1)S(1)} %pad_maximum_fusion), channel_id=1, source_target_pairs={{0,2},{1,5},{2,0},{3,7},{4,6},{5,1},{6,4},{7,3},{8,10},{9,13},{10,... | collective-permute-start | bytes 786440 | tf_op jit(solution)/shard_map/ppermute | solution.py:155
  14.2 7.1 %collective-permute-start.4 = (bf16[4,2,32,512]{3,2,1,0:T(8,128)(2,1)S(1)}, bf16[4,2,32,512]{3,2,1,0:T(8,128)(2,1)S(1)}, u32[]{:S(2)}, u32[]{:S(2)}) collective-permute-start(bf16[4,2,32,512]{3,2,1,0:T(8,128)(2,1)S(1)} %pad_maximum_fusion), channel_id=1, source_target_pairs={{0,4},{1,3},{2,6},{3,1},{4,0},{5,7},{6,2},{7,5},{8,12},{9,11},{10,... | collective-permute-start | bytes 786440 | tf_op jit(solution)/shard_map/ppermute | solution.py:155
  16.5 1.6 %copy-start.1 = (bf16[1,4,512,512]{3,2,1,0:T(8,128)(2,1)S(1)}, bf16[1,4,512,512]{3,2,1,0:T(8,128)(2,1)}, u32[]{:S(2)}) copy-start(bf16[1,4,512,512]{3,2,1,0:T(8,128)(2,1)} %right.1) | copy-start | bytes 6291460
  18.1 1.2 %copy-start.2 = (bf16[1,2,512,512]{3,2,1,0:T(8,128)(2,1)S(1)}, bf16[1,2,512,512]{3,2,1,0:T(8,128)(2,1)}, u32[]{:S(2)}) copy-start(bf16[1,2,512,512]{3,2,1,0:T(8,128)(2,1)} %left.1) | copy-start | bytes 3145732
  21.4 8.1 %copy-start.3 = (s32[1,1,12]{2,1,0:T(1,128)S(1)}, s32[1,1,12]{2,1,0:T(1,128)}, u32[]{:S(2)}) copy-start(s32[1,1,12]{2,1,0:T(1,128)} %pairs.5) | copy-start | bytes 148
  21.4 8.1 %copy-start.4 = (s32[1,1,12]{2,1,0:T(1,128)S(1)}, s32[1,1,12]{2,1,0:T(1,128)}, u32[]{:S(2)}) copy-start(s32[1,1,12]{2,1,0:T(1,128)} %targets.5) | copy-start | bytes 148
  21.4 2.4 %collective-permute-start.6 = (bf16[12,2,32,512]{3,2,1,0:T(8,128)(2,1)S(1)}, bf16[12,2,32,512]{3,2,1,0:T(8,128)(2,1)S(1)}, u32[]{:S(2)}, u32[]{:S(2)}) collective-permute-start(bf16[12,2,32,512]{3,2,1,0:T(8,128)(2,1)S(1)} %constant_dynamic-update-slice_fusion.mine), channel_id=1, source_target_pairs={{0,1},{1,0},{2,3},{3,2},{4,5},{5,4},{6,7},{7,6},{8,9},{9,8},{10,11... | collective-permute-start | bytes 2359304 | tf_op jit(solution)/shard_map/ppermute | solution.py:181
  21.5 6.4 %collective-permute-start.5 = (bf16[4,2,32,512]{3,2,1,0:T(8,128)(2,1)S(1)}, bf16[4,2,32,512]{3,2,1,0:T(8,128)(2,1)S(1)}, u32[]{:S(2)}, u32[]{:S(2)}) collective-permute-start(bf16[4,2,32,512]{3,2,1,0:T(8,128)(2,1)S(1)} %collective-permute-done.3), channel_id=1, source_target_pairs={{0,4},{1,3},{2,6},{3,1},{4,0},{5,7},{6,2},{7,5},{8,12},{9,11},{10,... | collective-permute-start | bytes 786440 | tf_op jit(solution)/shard_map/ppermute | solution.py:155
  27.9 1.5 %collective-permute-start.7 = (bf16[4,2,32,512]{3,2,1,0:T(8,128)(2,1)S(1)}, bf16[4,2,32,512]{3,2,1,0:T(8,128)(2,1)S(1)}, u32[]{:S(2)}, u32[]{:S(2)}) collective-permute-start(bf16[4,2,32,512]{3,2,1,0:T(8,128)(2,1)S(1)} %collective-permute-done.5.mine_last), channel_id=1, source_target_pairs={{0,1},{1,0},{2,3},{3,2},{4,5},{5,4},{6,7},{7,6},{8,9},{9,8},{10,11... | collective-permute-start | bytes 786440 | tf_op jit(solution)/shard_map/ppermute | solution.py:189
  31.4 6.8 %collective-permute-start.9 = (bf16[4,2,32,512]{3,2,1,0:T(8,128)(2,1)S(1)}, bf16[4,2,32,512]{3,2,1,0:T(8,128)(2,1)S(1)}, u32[]{:S(2)}, u32[]{:S(2)}) collective-permute-start(bf16[4,2,32,512]{3,2,1,0:T(8,128)(2,1)S(1)} %get-tuple-element.68), channel_id=1, source_target_pairs={{0,2},{1,5},{2,0},{3,7},{4,6},{5,1},{6,4},{7,3},{8,10},{9,13},{10,... | collective-permute-start | bytes 786440 | tf_op jit(solution)/shard_map/ppermute | solution.py:155
  33.8 6.8 %collective-permute-start.8 = (bf16[4,2,32,512]{3,2,1,0:T(8,128)(2,1)S(1)}, bf16[4,2,32,512]{3,2,1,0:T(8,128)(2,1)S(1)}, u32[]{:S(2)}, u32[]{:S(2)}) collective-permute-start(bf16[4,2,32,512]{3,2,1,0:T(8,128)(2,1)S(1)} %shard_map.77), channel_id=1, source_target_pairs={{0,2},{1,5},{2,0},{3,7},{4,6},{5,1},{6,4},{7,3},{8,10},{9,13},{10,... | collective-permute-start | bytes 786440 | tf_op jit(solution)/shard_map/ppermute | solution.py:155
  38.3 5.7 %collective-permute-start.10 = (bf16[3,2,32,512]{3,2,1,0:T(8,128)(2,1)S(1)}, bf16[3,2,32,512]{3,2,1,0:T(8,128)(2,1)S(1)}, u32[]{:S(2)}, u32[]{:S(2)}) collective-permute-start(bf16[3,2,32,512]{3,2,1,0:T(8,128)(2,1)S(1)} %slice.38), channel_id=1, source_target_pairs={{0,4},{1,3},{2,6},{3,1},{4,0},{5,7},{6,2},{7,5},{8,12},{9,11},{10,... | collective-permute-start | bytes 589832 | tf_op jit(solution)/shard_map/ppermute | solution.py:155
  44.2 6.3 %collective-permute-start.12 = (bf16[2,32,512]{2,1,0:T(8,128)(2,1)S(1)}, bf16[2,32,512]{2,1,0:T(8,128)(2,1)S(1)}, u32[]{:S(2)}, u32[]{:S(2)}) collective-permute-start(bf16[2,32,512]{2,1,0:T(8,128)(2,1)S(1)} %get-tuple-element.71), channel_id=1, source_target_pairs={{0,16},{1,17},{2,18},{3,19},{4,20},{5,21},{6,22},{7,23},{8,24},{9,... | collective-permute-start | bytes 196616 | tf_op jit(solution)/shard_map/ppermute | solution.py:155
  45.8 6.1 %collective-permute-start.13 = (bf16[2,32,512]{2,1,0:T(8,128)(2,1)S(1)}, bf16[2,32,512]{2,1,0:T(8,128)(2,1)S(1)}, u32[]{:S(2)}, u32[]{:S(2)}) collective-permute-start(bf16[2,32,512]{2,1,0:T(8,128)(2,1)S(1)} %get-tuple-element.73), channel_id=1, source_target_pairs={{0,24},{1,25},{2,26},{3,27},{4,28},{5,29},{6,30},{7,31},{8,16},{9,... | collective-permute-start | bytes 196616 | tf_op jit(solution)/shard_map/ppermute | solution.py:155
  46.5 5.4 %collective-permute-start.14 = (bf16[2,32,512]{2,1,0:T(8,128)(2,1)S(1)}, bf16[2,32,512]{2,1,0:T(8,128)(2,1)S(1)}, u32[]{:S(2)}, u32[]{:S(2)}) collective-permute-start(bf16[2,32,512]{2,1,0:T(8,128)(2,1)S(1)} %get-tuple-element.72), channel_id=1, source_target_pairs={{0,8},{1,9},{2,10},{3,11},{4,12},{5,13},{6,14},{7,15},{8,0},{9,1},... | collective-permute-start | bytes 196616 | tf_op jit(solution)/shard_map/ppermute | solution.py:155
  47.7 4.3 %collective-permute-start.11 = (bf16[2,32,512]{2,1,0:T(8,128)(2,1)S(1)}, bf16[2,32,512]{2,1,0:T(8,128)(2,1)S(1)}, u32[]{:S(2)}, u32[]{:S(2)}) collective-permute-start(bf16[2,32,512]{2,1,0:T(8,128)(2,1)S(1)} %slice_bitcast_fusion), channel_id=1, source_target_pairs={{0,4},{1,3},{2,6},{3,1},{4,0},{5,7},{6,2},{7,5},{8,12},{9,11},{10,... | collective-permute-start | bytes 196616 | tf_op jit(solution)/shard_map/ppermute | solution.py:155

commit v5 on v4

--- a/solution.py
+++ b/solution.py
@@ -14,7 +14,7 @@
 VMEM = pl.BlockSpec(memory_space=pltpu.VMEM)
 SMEM = pl.BlockSpec(memory_space=pltpu.SMEM)
 SPARE_BYTES = 4 * 2**20
-GROUPS = ((3,), (1,), (2, 0))
+GROUPS = ((3,), (1,), (2,), (0,))
 
 
 def block_rows(me, core, quarter, level, rows):
@@ -202,10 +202,12 @@
     far = swap(far, first)
     near, = sums(next_kernel, 1, [], (BF16,), pairs, targets, live, early[1], lasts[1], wave_last, turned)
     near = swap(near, first)
-    passing, keep = sums(next_kernel, 2, [], (F32, F32), pairs, targets, live, early[2], lasts[2], wave_last, turned)
+    passing, = sums(next_kernel, 2, [], (F32,), pairs, targets, live, early[2], lasts[2], wave_last, turned)
 
     passing = (passing + far.astype(F32)).astype(BF16)
-    pass_rest = swap(passing[1:], second)
+    pass_rest, wave_last = lax.optimization_barrier((passing[1:], wave_last))
+    pass_rest = swap(pass_rest, second)
+    keep, = sums(next_kernel, 3, [], (F32,), pairs, targets, live, early[3], lasts[3], wave_last, turned)
     line_rest = (keep[1:] + near[1:].astype(F32) + pass_rest.astype(F32)).astype(BF16)
     line_rest, pass_own = lax.optimization_barrier((line_rest, passing[0]))
     arrived = [swap(line_rest[k - 1], none, k) for k in far_first]

time: 52.9 us -> 52.6 us (level)
  Pallas kernels: 10.4 us -> 11.4 us
  waiting for transfers between devices: 19 us -> 18.1 us
    ppermute x13, waiting for transfers between devices: 16.7 us -> 15.7 us  [swap(): return lax.ppermute(array, AXES, pairs_of)]
    pallas_call x5 -> x6, Pallas kernels: 10.4 us -> 11.4 us  [call(): pl.pallas_call(kernel, out_shape=out_shapes, in_specs=[spec(operand) for...]
  transfers between devices with their start and end apart: 15 -> 15, of which waited for: 10 -> 10; matrix products, arithmetic and copies ran while one was open for 2% -> 2% of each run, Pallas kernels for 16% -> 18%
where the time goes in v5:
time: 52.6 us; the launch traced here: 52.4 us
  waiting for transfers between devices  18.1 us (34%)
  starting transfers between devices  16.5 us (31%)
  Pallas kernels  11.4 us (22%)
  local copies, waits for them, and re-layouts  4.59 us (9%)
  other arithmetic  0.99 us (2%)
  between operations  0.82 us (2%)
    ppermute x13, starting transfers between devices, swap(): return lax.ppermute(array, AXES, pairs_of)  16.5 us
    ppermute x13, waiting for transfers between devices, swap(): return lax.ppermute(array, AXES, pairs_of)  15.7 us
    pallas_call x6, Pallas kernels, call(): pl.pallas_call(kernel, out_shape=out_shapes, in_specs=[spec(operand) for...  11.4 us
    unnamed x13, local copies, waits for them, and re-layouts  4.52 us
    ppermute x1, waiting for transfers between devices, on_device(): other = lax.ppermute(mine, AXES, across)  1.56 us
  transfers between devices with their start and end apart: 15, of which 10 were waited for; matrix products, arithmetic and copies ran while one was open for 2% of the time, Pallas kernels for 18%

profile of v5, /device:TPU:0, one launch (start us, length us, event | category | flops | bytes accessed | tf_op | source)
XLA Modules:
  0.0 52.4 jit_solution(13559422200741912836)
XLA Ops:
  0.0 0.9 %copy-done = bf16[4,32,512]{2,1,0:T(8,128)(2,1)S(1)} copy-done((bf16[4,32,512]{2,1,0:T(8,128)(2,1)S(1)}, bf16[4,32,512]{2,1,0:T(8,128)(2,1)}, u32[]{:S(2)}) %copy-start) | copy-done | bytes 131096
  0.9 3.0 %collective-permute-start = (bf16[1,2,32,512]{3,2,1,0:T(8,128)(2,1)S(1)}, bf16[1,2,32,512]{3,2,1,0:T(8,128)(2,1)S(1)}, u32[]{:S(2)}, u32[]{:S(2)}) collective-permute-start(bf16[1,2,32,512]{3,2,1,0:T(8,128)(2,1)S(1)} %dynamic-slice_bitcast_fusion), channel_id=1, source_target_pairs={{0,8},{1,9},{2,10},{3,11},{4,12},{5,13},{6,14},{7,15},{8,0},{9,1},... | collective-permute-start | bytes 196616 | tf_op jit(solution)/shard_map/ppermute | solution.py:155
  3.9 2.6 %collective-permute-start.1 = (bf16[1,2,32,512]{3,2,1,0:T(8,128)(2,1)S(1)}, bf16[1,2,32,512]{3,2,1,0:T(8,128)(2,1)S(1)}, u32[]{:S(2)}, u32[]{:S(2)}) collective-permute-start(bf16[1,2,32,512]{3,2,1,0:T(8,128)(2,1)S(1)} %dynamic-slice_bitcast_fusion), channel_id=1, source_target_pairs={{0,16},{1,17},{2,18},{3,19},{4,20},{5,21},{6,22},{7,23},{8,24},{9,... | collective-permute-start | bytes 196616 | tf_op jit(solution)/shard_map/ppermute | solution.py:155
  6.6 4.6 %collective-permute-done.1 = bf16[1,2,32,512]{3,2,1,0:T(8,128)(2,1)S(1)} collective-permute-done((bf16[1,2,32,512]{3,2,1,0:T(8,128)(2,1)S(1)}, bf16[1,2,32,512]{3,2,1,0:T(8,128)(2,1)S(1)}, u32[]{:S(2)}, u32[]{:S(2)}) %collective-permute-start.1) | collective-permute-done | bytes 65568 | tf_op jit(solution)/shard_map/ppermute | solution.py:155
  11.2 1.4 %collective-permute-done.2 = bf16[1,2,32,512]{3,2,1,0:T(8,128)(2,1)S(1)} collective-permute-done((bf16[1,2,32,512]{3,2,1,0:T(8,128)(2,1)S(1)}, bf16[1,2,32,512]{3,2,1,0:T(8,128)(2,1)S(1)}, u32[]{:S(2)}, u32[]{:S(2)}) %collective-permute-start.2) | collective-permute-done | bytes 65568 | tf_op jit(solution)/shard_map/ppermute | solution.py:155
  12.6 1.6 %collective-permute-start.3 = (bf16[4,2,32,512]{3,2,1,0:T(8,128)(2,1)S(1)}, bf16[4,2,32,512]{3,2,1,0:T(8,128)(2,1)S(1)}, u32[]{:S(2)}, u32[]{:S(2)}) collective-permute-start(bf16[4,2,32,512]{3,2,1,0:T(8,128)(2,1)S(1)} %pad_maximum_fusion), channel_id=1, source_target_pairs={{0,2},{1,5},{2,0},{3,7},{4,6},{5,1},{6,4},{7,3},{8,10},{9,13},{10,... | collective-permute-start | bytes 786440 | tf_op jit(solution)/shard_map/ppermute | solution.py:155
  14.2 1.5 %collective-permute-start.4 = (bf16[4,2,32,512]{3,2,1,0:T(8,128)(2,1)S(1)}, bf16[4,2,32,512]{3,2,1,0:T(8,128)(2,1)S(1)}, u32[]{:S(2)}, u32[]{:S(2)}) collective-permute-start(bf16[4,2,32,512]{3,2,1,0:T(8,128)(2,1)S(1)} %pad_maximum_fusion), channel_id=1, source_target_pairs={{0,4},{1,3},{2,6},{3,1},{4,0},{5,7},{6,2},{7,5},{8,12},{9,11},{10,... | collective-permute-start | bytes 786440 | tf_op jit(solution)/shard_map/ppermute | solution.py:155
  16.5 1.6 %copy-done.1 = bf16[1,4,512,512]{3,2,1,0:T(8,128)(2,1)S(1)} copy-done((bf16[1,4,512,512]{3,2,1,0:T(8,128)(2,1)S(1)}, bf16[1,4,512,512]{3,2,1,0:T(8,128)(2,1)}, u32[]{:S(2)}) %copy-start.1) | copy-done | bytes 2097176
  18.1 1.2 %copy-done.2 = bf16[1,2,512,512]{3,2,1,0:T(8,128)(2,1)S(1)} copy-done((bf16[1,2,512,512]{3,2,1,0:T(8,128)(2,1)S(1)}, bf16[1,2,512,512]{3,2,1,0:T(8,128)(2,1)}, u32[]{:S(2)}) %copy-start.2) | copy-done | bytes 1048600
  19.3 2.1 %shard_map.73 = (bf16[2,128,512]{2,1,0:T(8,128)(2,1)S(1)}, bf16[2,128,512]{2,1,0:T(8,128)(2,1)S(1)}, bf16[2,128,512]{2,1,0:T(8,128)(2,1)S(1)}, bf16[2,128,512]{2...) custom-call(s32[2]{0:T(128)S(1)} %pad_add_fusion.place, ...), custom_call_target="tpu_custom_call" | custom-call | flops 134217728 | bytes 1048576 | tf_op jit(solution)/shard_map/pallas_call | solution.py:128
  22.3 1.6 %collective-permute-done.6.other = bf16[12,2,32,512]{3,2,1,0:T(8,128)(2,1)S(1)} collective-permute-done((bf16[12,2,32,512]{3,2,1,0:T(8,128)(2,1)S(1)}, bf16[12,2,32,512]{3,2,1,0:T(8,128)(2,1)S(1)}, u32[]{:S(2)}, u32[]{:S(2)}) %collective-permute-start.6) | collective-permute-done | bytes 786464 | tf_op jit(solution)/shard_map/ppermute | solution.py:181
  23.9 1.9 %shard_map.74 = (f32[4,128,512]{2,1,0:T(8,128)S(1)}, f32[4,128,512]{2,1,0:T(8,128)S(1)}, f32[4,128,512]{2,1,0:T(8,128)S(1)}, f32[4,128,512]{2,1,0:T(8,128)S(1)}) custom-call(s32[4]{0:T(128)S(1)} %get-tuple-element.57.sources, bf16[12,2,32,512]{3,2,1,0:T(8,128)(2,1)S(1)} %constant_dynamic-update-slice_fusion.mine, ...), custom_call_target="tpu_custom_call" | custom-call | flops 1073741824 | bytes 1048576 | tf_op jit(solution)/shard_map/pallas_call | solution.py:128
  25.8 2.3 %collective-permute-done.5.mine_last = bf16[4,2,32,512]{3,2,1,0:T(8,128)(2,1)S(1)} collective-permute-done((bf16[4,2,32,512]{3,2,1,0:T(8,128)(2,1)S(1)}, bf16[4,2,32,512]{3,2,1,0:T(8,128)(2,1)S(1)}, u32[]{:S(2)}, u32[]{:S(2)}) %collective-permute-start.5) | collective-permute-done | bytes 262176 | tf_op jit(solution)/shard_map/ppermute | solution.py:155
  28.7 0.9 %collective-permute-done.7.other_last = bf16[4,2,32,512]{3,2,1,0:T(8,128)(2,1)S(1)} collective-permute-done((bf16[4,2,32,512]{3,2,1,0:T(8,128)(2,1)S(1)}, bf16[4,2,32,512]{3,2,1,0:T(8,128)(2,1)S(1)}, u32[]{:S(2)}, u32[]{:S(2)}) %collective-permute-start.7) | collective-permute-done | bytes 262176 | tf_op jit(solution)/shard_map/ppermute | solution.py:189
  29.6 1.9 %shard_map.75 = (bf16[2,128,512]{2,1,0:T(8,128)(2,1)S(1)}, bf16[4,2,32,512]{3,2,1,0:T(8,128)(2,1)S(1)}) custom-call(s32[4]{0:T(128)S(1)} %get-tuple-element.57.sources, s32[1,1,12]{2,1,0:T(1,128)S(1)} %copy-done.3, s32[1,1,12]{2,1,0:T(1,128)S(1)} %copy-done.4, s32[1,1]{1,0:T(1,128)S(6)} %copy.11.live, ...), custom_call_target="tpu_custom_call" | custom-call | flops 805306368 | bytes 1048576 | tf_op jit(solution)/shard_map/pallas_call | solution.py:128
  32.1 1.8 %shard_map.78 = bf16[4,2,32,512]{3,2,1,0:T(8,128)(2,1)S(1)} custom-call(s32[1,1,12]{2,1,0:T(1,128)S(1)} %copy-done.3, s32[1,1,12]{2,1,0:T(1,128)S(1)} %copy-done.4, s32[1,1]{1,0:T(1,128)S(6)} %copy.11.live, f32[4,128,512]{2,1,0:T(8,128)S(1)} %get-tuple-element.78.early, bf16[2,128,128]{2,1,0:T(8,128)(2,1)S(1)} %get-tuple-element.79.left_last, ...), custom_call_target="tpu_custom_call" | custom-call | flops 805306368 | bytes 1048576 | tf_op jit(solution)/shard_map/pallas_call | solution.py:128
  33.9 1.6 %collective-permute-start.9 = (bf16[4,2,32,512]{3,2,1,0:T(8,128)(2,1)S(1)}, bf16[4,2,32,512]{3,2,1,0:T(8,128)(2,1)S(1)}, u32[]{:S(2)}, u32[]{:S(2)}) collective-permute-start(bf16[4,2,32,512]{3,2,1,0:T(8,128)(2,1)S(1)} %shard_map.78), channel_id=1, source_target_pairs={{0,2},{1,5},{2,0},{3,7},{4,6},{5,1},{6,4},{7,3},{8,10},{9,13},{10,... | collective-permute-start | bytes 786440 | tf_op jit(solution)/shard_map/ppermute | solution.py:155
  35.5 1.8 %shard_map.76 = f32[4,2,32,512]{3,2,1,0:T(8,128)S(1)} custom-call(s32[1,1,12]{2,1,0:T(1,128)S(1)} %copy-done.3, s32[1,1,12]{2,1,0:T(1,128)S(1)} %copy-done.4, s32[1,1]{1,0:T(1,128)S(6)} %copy.11.live, f32[4,128,512]{2,1,0:T(8,128)S(1)} %get-tuple-element.69.early, bf16[2,128,128]{2,1,0:T(8,128)(2,1)S(1)} %get-tuple-element.70.left_last, ...), custom_call_target="tpu_custom_call" | custom-call | flops 805306368 | bytes 1048576 | tf_op jit(solution)/shard_map/pallas_call | solution.py:128
  38.7 1.8 %shard_map.77 = f32[4,2,32,512]{3,2,1,0:T(8,128)S(1)} custom-call(s32[1,1,12]{2,1,0:T(1,128)S(1)} %copy-done.3, s32[1,1,12]{2,1,0:T(1,128)S(1)} %copy-done.4, s32[1,1]{1,0:T(1,128)S(6)} %copy.11.live, f32[4,128,512]{2,1,0:T(8,128)S(1)} %get-tuple-element.67.early, bf16[2,128,128]{2,1,0:T(8,128)(2,1)S(1)} %get-tuple-element.68.left_last, ...), custom_call_target="tpu_custom_call" | custom-call | flops 805306368 | bytes 1048576 | tf_op jit(solution)/shard_map/pallas_call | solution.py:128
  41.4 2.3 %collective-permute-done.10 = bf16[3,2,32,512]{3,2,1,0:T(8,128)(2,1)S(1)} collective-permute-done((bf16[3,2,32,512]{3,2,1,0:T(8,128)(2,1)S(1)}, bf16[3,2,32,512]{3,2,1,0:T(8,128)(2,1)S(1)}, u32[]{:S(2)}, u32[]{:S(2)}) %collective-permute-start.10) | collective-permute-done | bytes 196640 | tf_op jit(solution)/shard_map/ppermute | solution.py:155
  43.9 1.7 %collective-permute-start.12 = (bf16[2,32,512]{2,1,0:T(8,128)(2,1)S(1)}, bf16[2,32,512]{2,1,0:T(8,128)(2,1)S(1)}, u32[]{:S(2)}, u32[]{:S(2)}) collective-permute-start(bf16[2,32,512]{2,1,0:T(8,128)(2,1)S(1)} %get-tuple-element.83), channel_id=1, source_target_pairs={{0,16},{1,17},{2,18},{3,19},{4,20},{5,21},{6,22},{7,23},{8,24},{9,... | collective-permute-start | bytes 196616 | tf_op jit(solution)/shard_map/ppermute | solution.py:155
  46.2 1.3 %collective-permute-start.14 = (bf16[2,32,512]{2,1,0:T(8,128)(2,1)S(1)}, bf16[2,32,512]{2,1,0:T(8,128)(2,1)S(1)}, u32[]{:S(2)}, u32[]{:S(2)}) collective-permute-start(bf16[2,32,512]{2,1,0:T(8,128)(2,1)S(1)} %get-tuple-element.84), channel_id=1, source_target_pairs={{0,8},{1,9},{2,10},{3,11},{4,12},{5,13},{6,14},{7,15},{8,0},{9,1},... | collective-permute-start | bytes 196616 | tf_op jit(solution)/shard_map/ppermute | solution.py:155
  48.1 2.5 %collective-permute-done.12 = bf16[2,32,512]{2,1,0:T(8,128)(2,1)S(1)} collective-permute-done((bf16[2,32,512]{2,1,0:T(8,128)(2,1)S(1)}, bf16[2,32,512]{2,1,0:T(8,128)(2,1)S(1)}, u32[]{:S(2)}, u32[]{:S(2)}) %collective-permute-start.12) | collective-permute-done | bytes 65568 | tf_op jit(solution)/shard_map/ppermute | solution.py:155
  50.6 1.1 %collective-permute-done.13 = bf16[2,32,512]{2,1,0:T(8,128)(2,1)S(1)} collective-permute-done((bf16[2,32,512]{2,1,0:T(8,128)(2,1)S(1)}, bf16[2,32,512]{2,1,0:T(8,128)(2,1)S(1)}, u32[]{:S(2)}, u32[]{:S(2)}) %collective-permute-start.13) | collective-permute-done | bytes 65568 | tf_op jit(solution)/shard_map/ppermute | solution.py:155
  (35 shorter events, 6.7 us)
Async XLA Ops:
  0.0 0.9 %copy-start = (bf16[4,32,512]{2,1,0:T(8,128)(2,1)S(1)}, bf16[4,32,512]{2,1,0:T(8,128)(2,1)}, u32[]{:S(2)}) copy-start(bf16[4,32,512]{2,1,0:T(8,128)(2,1)} %param.7) | copy-start | bytes 393220
  0.9 5.7 %collective-permute-start = (bf16[1,2,32,512]{3,2,1,0:T(8,128)(2,1)S(1)}, bf16[1,2,32,512]{3,2,1,0:T(8,128)(2,1)S(1)}, u32[]{:S(2)}, u32[]{:S(2)}) collective-permute-start(bf16[1,2,32,512]{3,2,1,0:T(8,128)(2,1)S(1)} %dynamic-slice_bitcast_fusion), channel_id=1, source_target_pairs={{0,8},{1,9},{2,10},{3,11},{4,12},{5,13},{6,14},{7,15},{8,0},{9,1},... | collective-permute-start | bytes 196616 | tf_op jit(solution)/shard_map/ppermute | solution.py:155
  3.9 7.3 %collective-permute-start.1 = (bf16[1,2,32,512]{3,2,1,0:T(8,128)(2,1)S(1)}, bf16[1,2,32,512]{3,2,1,0:T(8,128)(2,1)S(1)}, u32[]{:S(2)}, u32[]{:S(2)}) collective-permute-start(bf16[1,2,32,512]{3,2,1,0:T(8,128)(2,1)S(1)} %dynamic-slice_bitcast_fusion), channel_id=1, source_target_pairs={{0,16},{1,17},{2,18},{3,19},{4,20},{5,21},{6,22},{7,23},{8,24},{9,... | collective-permute-start | bytes 196616 | tf_op jit(solution)/shard_map/ppermute | solution.py:155
  6.5 6.1 %collective-permute-start.2 = (bf16[1,2,32,512]{3,2,1,0:T(8,128)(2,1)S(1)}, bf16[1,2,32,512]{3,2,1,0:T(8,128)(2,1)S(1)}, u32[]{:S(2)}, u32[]{:S(2)}) collective-permute-start(bf16[1,2,32,512]{3,2,1,0:T(8,128)(2,1)S(1)} %dynamic-slice_bitcast_fusion), channel_id=1, source_target_pairs={{0,24},{1,25},{2,26},{3,27},{4,28},{5,29},{6,30},{7,31},{8,16},{9,... | collective-permute-start | bytes 196616 | tf_op jit(solution)/shard_map/ppermute | solution.py:155
  12.6 8.8 %collective-permute-start.3 = (bf16[4,2,32,512]{3,2,1,0:T(8,128)(2,1)S(1)}, bf16[4,2,32,512]{3,2,1,0:T(8,128)(2,1)S(1)}, u32[]{:S(2)}, u32[]{:S(2)}) collective-permute-start(bf16[4,2,32,512]{3,2,1,0:T(8,128)(2,1)S(1)} %pad_maximum_fusion), channel_id=1, source_target_pairs={{0,2},{1,5},{2,0},{3,7},{4,6},{5,1},{6,4},{7,3},{8,10},{9,13},{10,... | collective-permute-start | bytes 786440 | tf_op jit(solution)/shard_map/ppermute | solution.py:155
  14.2 7.2 %collective-permute-start.4 = (bf16[4,2,32,512]{3,2,1,0:T(8,128)(2,1)S(1)}, bf16[4,2,32,512]{3,2,1,0:T(8,128)(2,1)S(1)}, u32[]{:S(2)}, u32[]{:S(2)}) collective-permute-start(bf16[4,2,32,512]{3,2,1,0:T(8,128)(2,1)S(1)} %pad_maximum_fusion), channel_id=1, source_target_pairs={{0,4},{1,3},{2,6},{3,1},{4,0},{5,7},{6,2},{7,5},{8,12},{9,11},{10,... | collective-permute-start | bytes 786440 | tf_op jit(solution)/shard_map/ppermute | solution.py:155
  16.5 1.6 %copy-start.1 = (bf16[1,4,512,512]{3,2,1,0:T(8,128)(2,1)S(1)}, bf16[1,4,512,512]{3,2,1,0:T(8,128)(2,1)}, u32[]{:S(2)}) copy-start(bf16[1,4,512,512]{3,2,1,0:T(8,128)(2,1)} %right.1) | copy-start | bytes 6291460
  18.1 1.2 %copy-start.2 = (bf16[1,2,512,512]{3,2,1,0:T(8,128)(2,1)S(1)}, bf16[1,2,512,512]{3,2,1,0:T(8,128)(2,1)}, u32[]{:S(2)}) copy-start(bf16[1,2,512,512]{3,2,1,0:T(8,128)(2,1)} %left.1) | copy-start | bytes 3145732
  21.5 8.1 %copy-start.3 = (s32[1,1,12]{2,1,0:T(1,128)S(1)}, s32[1,1,12]{2,1,0:T(1,128)}, u32[]{:S(2)}) copy-start(s32[1,1,12]{2,1,0:T(1,128)} %pairs.7) | copy-start | bytes 148
  21.5 8.1 %copy-start.4 = (s32[1,1,12]{2,1,0:T(1,128)S(1)}, s32[1,1,12]{2,1,0:T(1,128)}, u32[]{:S(2)}) copy-start(s32[1,1,12]{2,1,0:T(1,128)} %targets.7) | copy-start | bytes 148
  21.5 2.4 %collective-permute-start.6 = (bf16[12,2,32,512]{3,2,1,0:T(8,128)(2,1)S(1)}, bf16[12,2,32,512]{3,2,1,0:T(8,128)(2,1)S(1)}, u32[]{:S(2)}, u32[]{:S(2)}) collective-permute-start(bf16[12,2,32,512]{3,2,1,0:T(8,128)(2,1)S(1)} %constant_dynamic-update-slice_fusion.mine), channel_id=1, source_target_pairs={{0,1},{1,0},{2,3},{3,2},{4,5},{5,4},{6,7},{7,6},{8,9},{9,8},{10,11... | collective-permute-start | bytes 2359304 | tf_op jit(solution)/shard_map/ppermute | solution.py:181
  21.6 6.4 %collective-permute-start.5 = (bf16[4,2,32,512]{3,2,1,0:T(8,128)(2,1)S(1)}, bf16[4,2,32,512]{3,2,1,0:T(8,128)(2,1)S(1)}, u32[]{:S(2)}, u32[]{:S(2)}) collective-permute-start(bf16[4,2,32,512]{3,2,1,0:T(8,128)(2,1)S(1)} %collective-permute-done.3), channel_id=1, source_target_pairs={{0,4},{1,3},{2,6},{3,1},{4,0},{5,7},{6,2},{7,5},{8,12},{9,11},{10,... | collective-permute-start | bytes 786440 | tf_op jit(solution)/shard_map/ppermute | solution.py:155
  28.0 1.5 %collective-permute-start.7 = (bf16[4,2,32,512]{3,2,1,0:T(8,128)(2,1)S(1)}, bf16[4,2,32,512]{3,2,1,0:T(8,128)(2,1)S(1)}, u32[]{:S(2)}, u32[]{:S(2)}) collective-permute-start(bf16[4,2,32,512]{3,2,1,0:T(8,128)(2,1)S(1)} %collective-permute-done.5.mine_last), channel_id=1, source_target_pairs={{0,1},{1,0},{2,3},{3,2},{4,5},{5,4},{6,7},{7,6},{8,9},{9,8},{10,11... | collective-permute-start | bytes 786440 | tf_op jit(solution)/shard_map/ppermute | solution.py:189
  31.5 6.4 %collective-permute-start.8 = (bf16[4,2,32,512]{3,2,1,0:T(8,128)(2,1)S(1)}, bf16[4,2,32,512]{3,2,1,0:T(8,128)(2,1)S(1)}, u32[]{:S(2)}, u32[]{:S(2)}) collective-permute-start(bf16[4,2,32,512]{3,2,1,0:T(8,128)(2,1)S(1)} %get-tuple-element.76), channel_id=1, source_target_pairs={{0,2},{1,5},{2,0},{3,7},{4,6},{5,1},{6,4},{7,3},{8,10},{9,13},{10,... | collective-permute-start | bytes 786440 | tf_op jit(solution)/shard_map/ppermute | solution.py:155
  33.9 7.5 %collective-permute-start.9 = (bf16[4,2,32,512]{3,2,1,0:T(8,128)(2,1)S(1)}, bf16[4,2,32,512]{3,2,1,0:T(8,128)(2,1)S(1)}, u32[]{:S(2)}, u32[]{:S(2)}) collective-permute-start(bf16[4,2,32,512]{3,2,1,0:T(8,128)(2,1)S(1)} %shard_map.78), channel_id=1, source_target_pairs={{0,2},{1,5},{2,0},{3,7},{4,6},{5,1},{6,4},{7,3},{8,10},{9,13},{10,... | collective-permute-start | bytes 786440 | tf_op jit(solution)/shard_map/ppermute | solution.py:155
  38.0 5.7 %collective-permute-start.10 = (bf16[3,2,32,512]{3,2,1,0:T(8,128)(2,1)S(1)}, bf16[3,2,32,512]{3,2,1,0:T(8,128)(2,1)S(1)}, u32[]{:S(2)}, u32[]{:S(2)}) collective-permute-start(bf16[3,2,32,512]{3,2,1,0:T(8,128)(2,1)S(1)} %slice.36), channel_id=1, source_target_pairs={{0,4},{1,3},{2,6},{3,1},{4,0},{5,7},{6,2},{7,5},{8,12},{9,11},{10,... | collective-permute-start | bytes 589832 | tf_op jit(solution)/shard_map/ppermute | solution.py:155
  43.9 6.7 %collective-permute-start.12 = (bf16[2,32,512]{2,1,0:T(8,128)(2,1)S(1)}, bf16[2,32,512]{2,1,0:T(8,128)(2,1)S(1)}, u32[]{:S(2)}, u32[]{:S(2)}) collective-permute-start(bf16[2,32,512]{2,1,0:T(8,128)(2,1)S(1)} %get-tuple-element.83), channel_id=1, source_target_pairs={{0,16},{1,17},{2,18},{3,19},{4,20},{5,21},{6,22},{7,23},{8,24},{9,... | collective-permute-start | bytes 196616 | tf_op jit(solution)/shard_map/ppermute | solution.py:155
  45.5 6.2 %collective-permute-start.13 = (bf16[2,32,512]{2,1,0:T(8,128)(2,1)S(1)}, bf16[2,32,512]{2,1,0:T(8,128)(2,1)S(1)}, u32[]{:S(2)}, u32[]{:S(2)}) collective-permute-start(bf16[2,32,512]{2,1,0:T(8,128)(2,1)S(1)} %get-tuple-element.85), channel_id=1, source_target_pairs={{0,24},{1,25},{2,26},{3,27},{4,28},{5,29},{6,30},{7,31},{8,16},{9,... | collective-permute-start | bytes 196616 | tf_op jit(solution)/shard_map/ppermute | solution.py:155
  46.2 5.5 %collective-permute-start.14 = (bf16[2,32,512]{2,1,0:T(8,128)(2,1)S(1)}, bf16[2,32,512]{2,1,0:T(8,128)(2,1)S(1)}, u32[]{:S(2)}, u32[]{:S(2)}) collective-permute-start(bf16[2,32,512]{2,1,0:T(8,128)(2,1)S(1)} %get-tuple-element.84), channel_id=1, source_target_pairs={{0,8},{1,9},{2,10},{3,11},{4,12},{5,13},{6,14},{7,15},{8,0},{9,1},... | collective-permute-start | bytes 196616 | tf_op jit(solution)/shard_map/ppermute | solution.py:155
  47.4 4.3 %collective-permute-start.11 = (bf16[2,32,512]{2,1,0:T(8,128)(2,1)S(1)}, bf16[2,32,512]{2,1,0:T(8,128)(2,1)S(1)}, u32[]{:S(2)}, u32[]{:S(2)}) collective-permute-start(bf16[2,32,512]{2,1,0:T(8,128)(2,1)S(1)} %slice_bitcast_fusion), channel_id=1, source_target_pairs={{0,4},{1,3},{2,6},{3,1},{4,0},{5,7},{6,2},{7,5},{8,12},{9,11},{10,... | collective-permute-start | bytes 196616 | tf_op jit(solution)/shard_map/ppermute | solution.py:155
